TPU v7x, 32 devices: a whole 2x2x4 slice. The times are simulated.
32 devices in a mesh: group: 4 (over z), bulk: 8 (over y, x, core).
Axes of the slice: x: 2, y: 2, z: 4, core: 2. Of those that a mesh axis runs over, the one named last changes fastest.
Arguments:
- p_tiles: float32 [1536, 128, 128], P(('group', 'bulk')), may hold values from -0.5 to 0.5
- a_tiles: float32 [1536, 7, 128, 128], P(('group', 'bulk')), may hold values from -0.5 to 0.5
- col_ref: int32 [1536, 7], P(('group', 'bulk')), may hold values from 0 to 111, as said below
- send_list: int32 [32, 2, 32], P(('group', 'bulk')), may hold values from -1 to 47, as said below
- coarse_tile: int32 [1536, 7], P(('group', 'bulk')), may hold values from 0 to 127
Outputs:
- coarse_op: float32 [512, 128, 128], P('group')
Inputs may be any that keep to these rules, and one draw needn't show every extreme that they name: `send_list`: entry [s, 0, j] is the local index of a fine block of device s that device s - 1 receives in slot j, entry [s, 1, j] one that device s + 1 receives; the slots of one entry hold distinct blocks, filled slots come first, -1 marks an empty slot. Device 0 sends nothing below and the last device nothing above; every other pair fills between 16 and 32 slots, and device 0 fills all 32 slots for device 1. `col_ref`: on device d, a value v under 48 names d's own fine block v; a value v of 48 or more names the tile that d receives in slot (v - 48) % 32 from the slab below if (v - 48) // 32 is 0, from the slab above if it is 1, always a filled slot. Every filled slot that d receives is named by exactly one coupling of d.
All inputs are finite; a program needn't handle non-finite values.
Results may differ from a plain program's by a relative error of at most 0.0003.
Values sent between devices are 32-bit elements; how exact they have to be, the bound alone decides.
A program may use at most 192 MiB of HBM per device.

v0:
```python
import jax
import jax.numpy as jnp
from jax import lax
from jax.sharding import PartitionSpec as P

CT = 128


def shifted(block, axis, distance):
    devices = range(lax.axis_size(axis))
    route = [(i - distance, i) for i in devices if i - distance in devices]
    return lax.ppermute(block, axis, route)


def shards(p_tiles, a_tiles, col_ref, send_list, coarse_tile):
    blocks, cell_width, coarse = p_tiles.shape
    neighbours = a_tiles.shape[1]
    capacity = send_list.shape[2]
    outgoing = send_list[0].reshape(-1)
    chosen = jnp.take(p_tiles, jnp.maximum(outgoing, 0), axis=0)
    chosen = jnp.where((outgoing >= 0)[:, None, None], chosen, 0.0)
    chosen = chosen.reshape(2, capacity, cell_width, coarse)
    lower_tiles = shifted(chosen[1], ("group", "bulk"), 1)
    upper_tiles = shifted(chosen[0], ("group", "bulk"), -1)
    lookup_rows = jnp.concatenate([p_tiles, lower_tiles, upper_tiles], axis=0)
    right_tiles = jnp.take(lookup_rows, col_ref.reshape(-1), axis=0)
    couplings = a_tiles.reshape(blocks * neighbours, cell_width, cell_width)
    product = jnp.einsum("qxy,qyc->qxc", couplings, right_tiles, precision=lax.Precision.HIGHEST)
    triple = jnp.einsum(
        "ixa,ikxc->ikac",
        p_tiles,
        product.reshape(blocks, neighbours, cell_width, coarse),
        precision=lax.Precision.HIGHEST,
    )
    triple = triple.reshape(blocks * neighbours, coarse, coarse)
    tile_count = CT
    selector = (
        coarse_tile.reshape(-1)[None, :] == jnp.arange(tile_count, dtype=jnp.int32)[:, None]
    ).astype(jnp.float32)
    partial_op = jnp.einsum("sq,qac->sac", selector, triple, precision=lax.Precision.HIGHEST)
    operator = lax.psum(partial_op, "bulk")
    return operator


def solution(mesh):
    in_specs = (
        P(("group", "bulk"), None, None),
        P(("group", "bulk"), None, None, None),
        P(("group", "bulk"), None),
        P(("group", "bulk"), None, None),
        P(("group", "bulk"), None),
    )
    out_specs = P("group", None, None)
    return jax.shard_map(shards, mesh=mesh, in_specs=in_specs, out_specs=out_specs, check_vma=False)
```

profile of v0, /device:TPU:1, one launch (start us, length us, event | category | flops | bytes accessed | tf_op | source)
XLA Modules:
  0.0 346.7 jit_solution(2840805442350117643)
XLA Ops:
  6.5 0.0 all-reduce.2.cloned.1.call-start
  6.5 0.7 broadcast_compare_fusion.1
  7.2 0.7 broadcast_maximum_fusion
  7.9 0.1 ge.28
  8.0 0.1 le.29
  8.1 0.1 reshape.90
  8.2 4.7 %gather_fusion = f32[64,128,128]{2,1,0:T(8,128)} fusion(f32[48,128,128]{2,1,0:T(8,128)} %param.5, s32[1024]{0:T(1024)S(1)} %pad_clamp_fusion.1), kind=kCustom, calls=%fused_computation | custom fusion | bytes 8388864 | tf_op jit(solution)/shard_map/jit(_take)/gather | solution.py:20
  12.9 0.0 copy-start.1
  12.9 0.0 copy-start.2
  12.9 2.8 select_select_fusion
  15.7 2.3 fusion.12
  18.0 4.5 %collective-permute-start = (f32[32,128,128]{2,1,0:T(8,128)}, f32[32,128,128]{2,1,0:T(8,128)}, u32[]{:S(2)}, u32[]{:S(2)}) collective-permute-start(f32[32,128,128]{2,1,0:T(8,128)} %get-tuple-element.5), channel_id=1, source_target_pairs={{0,1},{1,2},{2,3},{3,4},{4,5},{5,6},{6,7},{7,8},{8,9},{9,10},{10,1... | collective-permute-start | bytes 6291464 | tf_op jit(solution)/shard_map/ppermute | solution.py:12
  22.5 1.9 collective-permute-start.1
  24.4 0.0 copy-done.1
  24.4 0.1 copy.10
  24.5 0.1 reshape.84
  24.7 0.1 reshape.83
  24.8 0.0 copy-done.2
  24.8 0.1 copy.9
  24.9 0.1 eq.15
  25.1 43.2 %collective-permute-done = f32[32,128,128]{2,1,0:T(8,128)} collective-permute-done((f32[32,128,128]{2,1,0:T(8,128)}, f32[32,128,128]{2,1,0:T(8,128)}, u32[]{:S(2)}, u32[]{:S(2)}) %collective-permute-start) | collective-permute-done | bytes 2097184 | tf_op jit(solution)/shard_map/ppermute | solution.py:12
  68.3 1.6 collective-permute-done.1
  69.9 0.0 copy-done
  69.9 5.1 %pad_maximum_fusion = f32[112,128,128]{2,1,0:T(8,128)} fusion(f32[32,128,128]{2,1,0:T(8,128)} %collective-permute-done.1, f32[32,128,128]{2,1,0:T(8,128)} %collective-permute-done, f32[48,128,128]{2,1,0:T(8,128)S(1)} %copy-done), kind=kLoop, calls=%fused_computation.6 | loop fusion | flops 3670016 | bytes 14680064 | tf_op jit(solution)/shard_map/concatenate | solution.py:25
  75.0 17.3 %gather_fusion.1 = f32[336,128,128]{2,1,0:T(8,128)} fusion(f32[112,128,128]{2,1,0:T(8,128)} %pad_maximum_fusion, s32[1024]{0:T(1024)S(1)} %pad_clamp_fusion), kind=kCustom, calls=%fused_computation.1 | custom fusion | bytes 44041536 | tf_op jit(solution)/shard_map/jit(_take)/gather | solution.py:26
  92.2 48.4 %fusion = f32[336,128,128]{2,1,0:T(8,128)} fusion(f32[336,128,128]{2,1,0:T(8,128)} %bitcast.20, f32[336,128,128]{2,1,0:T(8,128)} %gather_fusion.1, pred[336]{0:T(512)(128)(4,1)S(1)} %compare_and_fusion), kind=kOutput, calls=%fused_computation.2 | convolution fusion | flops 8461221888 | bytes 66060624 | tf_op jit(solution)/shard_map/qxy,qyc->qxc/dot_general | solution.py:28
  140.6 24.2 %fusion.4 = f32[48,7,128,128]{3,2,1,0:T(8,128)} fusion(f32[48,7,128,128]{2,3,1,0:T(8,128)} %bitcast.18, f32[48,128,128]{2,1,0:T(8,128)S(1)} %copy-done), kind=kOutput, calls=%fused_computation.8 | convolution fusion | flops 8455716864 | bytes 47185920 | tf_op jit(solution)/shard_map/ixa,ikxc->ikac/dot_general | solution.py:29
  164.9 21.8 %copy.13 = f32[336,128,128]{2,0,1:T(8,128)} copy(f32[336,128,128]{1,2,0:T(8,128)} %bitcast.19) | data formatting | bytes 44040192 | tf_op jit(solution)/shard_map/reshape | solution.py:35
  186.7 15.5 %fusion.7 = f32[128,128,128]{2,0,1:T(8,128)} fusion(f32[336,128,128]{2,0,1:T(8,128)} %copy.13, s32[336]{0:T(512)S(1)} %eq.15), kind=kOutput, calls=%fused_computation.12 | convolution fusion | flops 8455759872 | bytes 30410048 | tf_op jit(solution)/shard_map/sq,qac->sac/dot_general | solution.py:40
  202.2 0.0 all-reduce.2.cloned.1.call-update
  202.2 126.0 %all-reduce.2.cloned.1.call-done = f32[128,128,128]{2,0,1:T(8,128)} async-done(((f32[128,128,128]{2,0,1:T(8,128)}), f32[128,128,128]{2,0,1:T(8,128)}) %all-reduce.2.cloned.1.call-update) | async-done | bytes 8388624 | tf_op jit(solution)/shard_map/psum | solution.py:41
  328.2 11.6 %copy.14 = f32[128,128,128]{2,1,0:T(8,128)} copy(f32[128,128,128]{2,0,1:T(8,128)} %all-reduce.2.cloned.1.call-done) | data formatting | bytes 16777216 | tf_op jit(solution)/shard_map/psum | solution.py:41
  (5 shorter events, 0.0 us)
Async XLA Ops:
  6.5 321.7 %all-reduce.2.cloned.1.call-start = ((), (), s32[]{:S(2)}) async-start(), calls=%async_computation | async-start | bytes 16777216 | tf_op jit(solution)/shard_map/psum | solution.py:41
  12.9 11.6 %copy-start.1 = (s32[48,7]{0,1:T(8,128)S(1)}, s32[48,7]{0,1:T(8,128)}, u32[]{:S(2)}) copy-start(s32[48,7]{0,1:T(8,128)} %param.7) | copy-start | bytes 4036
  12.9 11.9 %copy-start.2 = (s32[48,7]{0,1:T(8,128)S(1)}, s32[48,7]{0,1:T(8,128)}, u32[]{:S(2)}) copy-start(s32[48,7]{0,1:T(8,128)} %param.9) | copy-start | bytes 4036
  12.9 57.0 %copy-start = (f32[48,128,128]{2,1,0:T(8,128)S(1)}, f32[48,128,128]{2,1,0:T(8,128)}, u32[]{:S(2)}) copy-start(f32[48,128,128]{2,1,0:T(8,128)} %param.5) | copy-start | bytes 9437188
  18.0 50.2 %collective-permute-start = (f32[32,128,128]{2,1,0:T(8,128)}, f32[32,128,128]{2,1,0:T(8,128)}, u32[]{:S(2)}, u32[]{:S(2)}) collective-permute-start(f32[32,128,128]{2,1,0:T(8,128)} %get-tuple-element.5), channel_id=1, source_target_pairs={{0,1},{1,2},{2,3},{3,4},{4,5},{5,6},{6,7},{7,8},{8,9},{9,10},{10,1... | collective-permute-start | bytes 6291464 | tf_op jit(solution)/shard_map/ppermute | solution.py:12
  22.5 47.4 %collective-permute-start.1 = (f32[32,128,128]{2,1,0:T(8,128)}, f32[32,128,128]{2,1,0:T(8,128)}, u32[]{:S(2)}, u32[]{:S(2)}) collective-permute-start(f32[32,128,128]{2,1,0:T(8,128)} %get-tuple-element.6), channel_id=1, source_target_pairs={{1,0},{2,1},{3,2},{4,3},{5,4},{6,5},{7,6},{8,7},{9,8},{10,9},{11,1... | collective-permute-start | bytes 6291464 | tf_op jit(solution)/shard_map/ppermute | solution.py:12
Sparse Core Ops, SparseCore 0:
  202.3 125.8 all-reduce.1
where the time goes:
time: 348 us; the launch traced here: 347 us
  waiting for transfers between devices  171 us (49%)
  matrix products  88.2 us (25%)
  local copies, waits for them, and re-layouts  58.5 us (17%)
  between operations  13.5 us (4%)
  other arithmetic  9.28 us (3%)
  starting transfers between devices  6.42 us (2%)
    psum x1, waiting for transfers between devices, shards(): operator = lax.psum(partial_op, 'bulk')  126 us
    dot_general x1, matrix products, shards(): jnp.einsum('qxy,qyc->qxc', couplings, right_tiles, precision=lax.Precisio...  48.4 us
    ppermute x2, waiting for transfers between devices, shifted(): return lax.ppermute(block, axis, route)  44.8 us
    dot_general x1, matrix products, shards(): jnp.einsum('ixa,ikxc->ikac', p_tiles, product.reshape(blocks, neighbours,...  24.2 us
    reshape x1, local copies, waits for them, and re-layouts, shards(): triple = triple.reshape(blocks * neighbours, coarse, coarse)  21.8 us
    gather x1, local copies, waits for them, and re-layouts, shards(): right_tiles = jnp.take(lookup_rows, col_ref.reshape(-1), axis=0)  17.3 us
    dot_general x1, matrix products, shards(): jnp.einsum('sq,qac->sac', selector, triple, precision=lax.Precision.HIGHEST)  15.5 us
    psum x1, local copies, waits for them, and re-layouts, shards(): operator = lax.psum(partial_op, 'bulk')  11.6 us
  transfers between devices with their start and end apart: 3, of which 3 were waited for; matrix products, arithmetic and copies ran while one was open for 0% of the time, Pallas kernels for 0%

commit v1 on v0

v1 whole, which is shorter than its diff:
```python
import functools

import jax
import jax.numpy as jnp
from jax import lax
from jax.experimental import pallas as pl
from jax.experimental.pallas import tpu as pltpu
from jax.sharding import PartitionSpec as P

CT = 128
STEP_BLOCKS = 4
CHUNKS = 8
VMEM_BYTES = 56 * 1024 * 1024


def shifted(block, axis, distance):
    devices = range(lax.axis_size(axis))
    route = [(i - distance, i) for i in devices if i - distance in devices]
    return lax.ppermute(block, axis, route)


def halves(x):
    high = x.astype(jnp.bfloat16)
    low = (x - high.astype(jnp.float32)).astype(jnp.bfloat16)
    return high, low


def left_form(x):
    return jnp.concatenate(halves(x), axis=1)


def right_form(x):
    row = jnp.concatenate(halves(x), axis=1)
    return jnp.concatenate([row, row], axis=0)


def product(left, right):
    both = jnp.dot(left, right, preferred_element_type=jnp.float32)
    width = both.shape[1] // 2
    return both[:, :width] + both[:, width:]


def pick_kernel(send_ref, p_ref, below_ref, above_ref, sem):
    capacity = send_ref.shape[2]

    def copy(side, j):
        target = below_ref if side == 0 else above_ref
        row = jnp.maximum(send_ref[0, side, j], 0)
        return pltpu.make_async_copy(p_ref.at[row], target.at[j], sem.at[side, j])

    for side in range(2):
        @pl.loop(0, capacity)
        def _(j):
            copy(side, j).start()
    for side in range(2):
        @pl.loop(0, capacity)
        def _(j):
            copy(side, j).wait()


def local_kernel(col_ref, tile_ref, p_ref, a_ref, sum_ref, left_ref, place_ref, right_p):
    blocks = p_ref.shape[0]
    neighbours = a_ref.shape[1]
    slots = left_ref.shape[0] - 1
    step = pl.program_id(0)

    @pl.when(step == 0)
    def _():
        @pl.loop(0, blocks)
        def _(f):
            right_p[f] = right_form(p_ref[f])

        @pl.loop(0, sum_ref.shape[0])
        def _(t):
            sum_ref[t] = jnp.zeros(sum_ref.shape[1:], jnp.float32)

        @pl.loop(0, slots + 1)
        def _(j):
            place_ref[j] = -1

    for i in range(STEP_BLOCKS):
        f = step * STEP_BLOCKS + i
        p_left = left_form(p_ref[f].T)
        for k in range(neighbours):
            v = col_ref[f, k]
            t = tile_ref[f, k]
            local = v < blocks
            slot = jnp.where(local, slots, v - blocks)
            left = product(p_left, right_form(a_ref[i, k]))
            left_cat = left_form(left)
            left_ref[slot] = left_cat
            place_ref[slot] = t
            triple = product(left_cat, right_p[jnp.minimum(v, blocks - 1)])
            sum_ref[t] += jnp.where(local, triple, 0.0)


def halo_kernel(place_ref, partial_ref, left_ref, lower_ref, upper_ref, sum_ref, sem):
    capacity = lower_ref.shape[0]
    load = pltpu.make_async_copy(partial_ref, sum_ref, sem)
    load.start()
    load.wait()
    for side, tiles in enumerate((lower_ref, upper_ref)):
        @pl.loop(0, capacity // 4)
        def _(group):
            for i in range(4):
                j = group * 4 + i
                place = place_ref[side * capacity + j]
                triple = product(left_ref[side * capacity + j], right_form(tiles[j]))
                sum_ref[jnp.maximum(place, 0)] += jnp.where(place >= 0, triple, 0.0)


def reduce_kernel(orders, part_ref, out_ref, mine, *rest):
    stages = len(orders[0])
    bufs = rest[:stages]
    load_sem, send_sem, recv_sem = rest[stages:]
    me = lax.axis_index("bulk")
    tiles = part_ref.shape[0]
    chunks = mine.shape[0]
    width = tiles // chunks
    ways = len(orders)
    bit = [(me // 2**b) % 2 for b in range(stages)]
    partner = [me + 2**b * (1 - 2 * bit[b]) for b in range(stages)]

    def load(c, way):
        first = orders[way][0]
        at = c * width + bit[first] * (width // 2)
        return pltpu.make_async_copy(part_ref.at[pl.ds(at, width // 2)], mine.at[c], load_sem.at[c])

    def keep(c, way, s):
        at = c * width
        size = width
        for level in range(s + 1):
            size //= 2
            at = at + bit[orders[way][level]] * size
        return at, size

    def scatter(c, way, s):
        b = orders[way][s]
        size = width >> (s + 1)
        if s == 0:
            src = part_ref.at[pl.ds(c * width + (1 - bit[b]) * size, size)]
        else:
            src = bufs[s - 1].at[c, pl.ds((1 - bit[b]) * size, size)]
        return pltpu.make_async_remote_copy(
            src_ref=src, dst_ref=bufs[s].at[c], send_sem=send_sem.at[s, c], recv_sem=recv_sem.at[s, c],
            device_id={"bulk": partner[b]}, device_id_type=pl.DeviceIdType.MESH)

    def gather(c, way, s):
        b = orders[way][s]
        at, size = keep(c, way, s)
        region = out_ref.at[pl.ds(at, size)]
        n = 2 * stages - 1 - s
        return pltpu.make_async_remote_copy(
            src_ref=region, dst_ref=region, send_sem=send_sem.at[n, c], recv_sem=recv_sem.at[n, c],
            device_id={"bulk": partner[b]}, device_id_type=pl.DeviceIdType.MESH)

    def add(c, way, s):
        b = orders[way][s]
        size = width >> (s + 1)
        at, _ = keep(c, way, s)

        @pl.loop(0, size)
        def _(j):
            if s == 0:
                own = mine[c, j]
            else:
                own = bufs[s - 1][c, bit[b] * size + j]
            total = bufs[s][c, j] + own
            if s == stages - 1:
                out_ref[at + j] = total
            else:
                bufs[s][c, j] = total

    def each(body):
        @pl.loop(0, chunks // ways)
        def _(g):
            for way in range(ways):
                body(g * ways + way, way)

    each(lambda c, way: load(c, way).start())
    barrier = pltpu.get_barrier_semaphore()
    for b in range(stages):
        pl.semaphore_signal(barrier, inc=1, device_id={"bulk": partner[b]}, device_id_type=pl.DeviceIdType.MESH)
    pl.semaphore_wait(barrier, stages)

    each(lambda c, way: scatter(c, way, 0).start())
    for s in range(stages):
        def reduce_step(c, way, s=s):
            if s == 0:
                load(c, way).wait()
            scatter(c, way, s).wait_recv()
            add(c, way, s)
            if s + 1 < stages:
                scatter(c, way, s + 1).start()
            else:
                gather(c, way, s).start()
        each(reduce_step)
    for s in reversed(range(stages)):
        def spread_step(c, way, s=s):
            gather(c, way, s).wait_recv()
            if s > 0:
                gather(c, way, s - 1).start()
        each(spread_step)

    def drain(c, way):
        for s in range(stages):
            scatter(c, way, s).wait_send()
            gather(c, way, s).wait_send()
    each(drain)


def group_sum(partial):
    devices = lax.axis_size("bulk")
    stages = devices.bit_length() - 1
    tiles, rows, columns = partial.shape
    width = tiles // CHUNKS
    bits = tuple(range(stages))
    if stages % 2:
        half = (stages - 1) // 2
        orders = (bits, bits[:1] + bits[1 + half:] + bits[1:1 + half])
    else:
        orders = (bits, bits[stages // 2:] + bits[:stages // 2])
    tile = (rows, columns)
    vmem = functools.partial(pltpu.VMEM, dtype=jnp.float32)
    return pl.pallas_call(
        functools.partial(reduce_kernel, orders),
        out_shape=jax.ShapeDtypeStruct(partial.shape, jnp.float32),
        in_specs=[pl.BlockSpec(memory_space=pl.ANY)],
        out_specs=pl.BlockSpec(memory_space=pltpu.VMEM),
        scratch_shapes=[vmem((CHUNKS, width // 2) + tile)]
        + [vmem((CHUNKS, width >> (s + 1)) + tile) for s in range(stages)]
        + [
            pltpu.SemaphoreType.DMA((CHUNKS,)),
            pltpu.SemaphoreType.DMA((2 * stages, CHUNKS)),
            pltpu.SemaphoreType.DMA((2 * stages, CHUNKS)),
        ],
        compiler_params=pltpu.CompilerParams(
            collective_id=0, has_side_effects=True, vmem_limit_bytes=VMEM_BYTES),
        cost_estimate=pl.CostEstimate(flops=tiles * rows * columns, bytes_accessed=8 * tiles * rows * columns, transcendentals=0),
        name="group_sum",
    )(partial)


def shards(p_tiles, a_tiles, col_ref, send_list, coarse_tile):
    blocks, rows, columns = p_tiles.shape
    neighbours = a_tiles.shape[1]
    capacity = send_list.shape[2]
    slots = 2 * capacity
    tile = (rows, columns)
    any_spec = pl.BlockSpec(memory_space=pl.ANY)
    smem_spec = pl.BlockSpec(memory_space=pltpu.SMEM)
    vmem_spec = pl.BlockSpec(memory_space=pltpu.VMEM)

    sent = jax.ShapeDtypeStruct((capacity,) + tile, jnp.float32)
    to_below, to_above = pl.pallas_call(
        pick_kernel,
        out_shape=(sent, sent),
        in_specs=[smem_spec, any_spec],
        out_specs=(any_spec, any_spec),
        scratch_shapes=[pltpu.SemaphoreType.DMA((2, capacity))],
        name="pick",
    )(send_list, p_tiles)
    lower = shifted(to_above, ("group", "bulk"), 1)
    upper = shifted(to_below, ("group", "bulk"), -1)

    couplings = blocks * neighbours
    whole = lambda *shape: pl.BlockSpec(shape, lambda s, *_: (0,) * len(shape))
    partial, left, place = pl.pallas_call(
        local_kernel,
        out_shape=(
            jax.ShapeDtypeStruct((CT,) + tile, jnp.float32),
            jax.ShapeDtypeStruct((slots + 1, rows, 2 * columns), jnp.bfloat16),
            jax.ShapeDtypeStruct((slots + 1,), jnp.int32),
        ),
        grid_spec=pltpu.PrefetchScalarGridSpec(
            num_scalar_prefetch=2,
            grid=(blocks // STEP_BLOCKS,),
            in_specs=[
                whole(blocks, *tile),
                pl.BlockSpec((STEP_BLOCKS, neighbours) + tile, lambda s, *_: (s, 0, 0, 0)),
            ],
            out_specs=(whole(CT, *tile), whole(slots + 1, rows, 2 * columns), pl.BlockSpec(memory_space=pltpu.SMEM)),
            scratch_shapes=[pltpu.VMEM((blocks, 2 * rows, 2 * columns), jnp.bfloat16)],
        ),
        compiler_params=pltpu.CompilerParams(vmem_limit_bytes=VMEM_BYTES),
        cost_estimate=pl.CostEstimate(
            flops=couplings * 16 * rows * rows * columns, bytes_accessed=4 * couplings * rows * columns, transcendentals=0),
        name="local_products",
    )(col_ref, coarse_tile, p_tiles, a_tiles)

    total = pl.pallas_call(
        halo_kernel,
        out_shape=jax.ShapeDtypeStruct((CT,) + tile, jnp.float32),
        in_specs=[smem_spec, any_spec, vmem_spec, vmem_spec, vmem_spec],
        out_specs=vmem_spec,
        scratch_shapes=[pltpu.SemaphoreType.DMA],
        compiler_params=pltpu.CompilerParams(vmem_limit_bytes=VMEM_BYTES),
        name="halo_products",
    )(place, partial, left, lower, upper)
    return group_sum(total)


def solution(mesh):
    in_specs = (
        P(("group", "bulk"), None, None),
        P(("group", "bulk"), None, None, None),
        P(("group", "bulk"), None),
        P(("group", "bulk"), None, None),
        P(("group", "bulk"), None),
    )
    out_specs = P("group", None, None)
    return jax.shard_map(shards, mesh=mesh, in_specs=in_specs, out_specs=out_specs, check_vma=False)
```

time: 348 us -> 283 us (0.81)
  Pallas kernels: 0 us -> 250 us
  waiting for transfers between devices: 171 us -> 15.5 us
  matrix products: 88.2 us -> 0 us
  local copies, waits for them, and re-layouts: 58.5 us -> 10.7 us
  between operations: 13.5 us -> 0.05 us
  other arithmetic: 9.28 us -> 0 us
    pallas_call x0 -> x4, Pallas kernels: none -> 250 us  [the longest x1 129 us: shards(): pl.pallas_call(pick_kernel, out_shape=(sent, sent), in_specs=[smem_spec,...]
    psum x1 -> x0, waiting for transfers between devices: 126 us -> none  [shards(): operator = lax.psum(partial_op, 'bulk')]
    dot_general x3 -> x0, matrix products: 88.2 us -> none  [the longest x1 48.4 us: shards(): jnp.einsum('qxy,qyc->qxc', couplings, right_tiles, precision=lax.Precisio...]
    ppermute x2, waiting for transfers between devices: 44.8 us -> 15.5 us  [shifted(): return lax.ppermute(block, axis, route)]
    reshape x3 -> x0, local copies, waits for them, and re-layouts: 22 us -> none  [the longest x1 21.8 us: shards(): triple = triple.reshape(blocks * neighbours, coarse, coarse)]
    gather x2 -> x0, local copies, waits for them, and re-layouts: 22 us -> none  [the longest x1 17.3 us: shards(): right_tiles = jnp.take(lookup_rows, col_ref.reshape(-1), axis=0)]
    psum x1 -> x0, local copies, waits for them, and re-layouts: 11.6 us -> none  [shards(): operator = lax.psum(partial_op, 'bulk')]
    unnamed x8 -> x5, local copies, waits for them, and re-layouts: 0.2 us -> 10.7 us
  transfers between devices with their start and end apart: 3 -> 2, of which waited for: 3 -> 2; matrix products, arithmetic and copies ran while one was open for 0% -> 1% of each run, Pallas kernels for 0% -> 10%
where the time goes in v1:
time: 283 us
  Pallas kernels  250 us (88%)
  waiting for transfers between devices  15.5 us (5%)
  local copies, waits for them, and re-layouts  10.7 us (4%)
  starting transfers between devices  6.43 us (2%)
    pallas_call x1, Pallas kernels, shards(): pl.pallas_call(pick_kernel, out_shape=(sent, sent), in_specs=[smem_spec,...  129 us
    pallas_call x1, Pallas kernels, group_sum(): pl.pallas_call(functools.partial(reduce_kernel, orders), out_shape=jax.Sh...  79.3 us
    pallas_call x1, Pallas kernels, shards(): pl.pallas_call(local_kernel, out_shape=(jax.ShapeDtypeStruct((CT,) + tile...  27.2 us
    ppermute x2, waiting for transfers between devices, shifted(): return lax.ppermute(block, axis, route)  15.5 us
    pallas_call x1, Pallas kernels, shards(): pl.pallas_call(halo_kernel, out_shape=jax.ShapeDtypeStruct((CT,) + tile,...  14 us
    unnamed x5, local copies, waits for them, and re-layouts  10.7 us
    ppermute x2, starting transfers between devices, shifted(): return lax.ppermute(block, axis, route)  6.43 us
  transfers between devices with their start and end apart: 2, of which 2 were waited for; matrix products, arithmetic and copies ran while one was open for 1% of the time, Pallas kernels for 10%

profile of v1, /device:TPU:1, one launch (start us, length us, event | category | flops | bytes accessed | tf_op | source)
XLA Modules:
  0.0 282.6 jit_solution(9310366785464844788)
XLA Ops:
  0.0 129.4 %pick.1 = (f32[32,128,128]{2,1,0:T(8,128)}, f32[32,128,128]{2,1,0:T(8,128)}) custom-call(s32[1,2,32]{2,1,0:T(2,128)} %send_ref.1, f32[48,128,128]{2,1,0:T(8,128)} %p_ref.3), custom_call_target="tpu_custom_call" | custom-call | tf_op jit(solution)/shard_map/pick/pallas_call | solution.py:255
  129.4 4.5 %collective-permute-start = (f32[32,128,128]{2,1,0:T(8,128)}, f32[32,128,128]{2,1,0:T(8,128)S(1)}, u32[]{:S(2)}, u32[]{:S(2)}) collective-permute-start(f32[32,128,128]{2,1,0:T(8,128)} %get-tuple-element.13), channel_id=1, source_target_pairs={{0,1},{1,2},{2,3},{3,4},{4,5},{5,6},{6,7},{7,8},{8,9},{9,10},{10,1... | collective-permute-start | bytes 6291464 | tf_op jit(solution)/shard_map/ppermute | solution.py:19
  133.9 1.9 collective-permute-start.1
  135.9 1.4 copy.6.col_ref
  137.3 1.4 copy.7.tile_ref
  138.6 27.2 %local_products.1 = (f32[128,128,128]{2,1,0:T(8,128)}, bf16[65,128,256]{2,1,0:T(8,128)(2,1)}, s32[65]{0:T(128)}) custom-call(s32[48,7]{1,0:T(8,128)} %copy.6.col_ref, s32[48,7]{1,0:T(8,128)} %copy.7.tile_ref, f32[48,128,128]{2,1,0:T(8,128)} %p_ref.3, f32[48,7,128,128]{3,2,1,0:T(8,128)} %a_ref.1), custom_call_target="tpu_custom_call" | custom-call | flops 11274289152 | bytes 22020096 | tf_op jit(solution)/shard_map/local_products/pallas_call | solution.py:268
  165.8 13.8 %collective-permute-done.lower_ref = f32[32,128,128]{2,1,0:T(8,128)S(1)} collective-permute-done((f32[32,128,128]{2,1,0:T(8,128)}, f32[32,128,128]{2,1,0:T(8,128)S(1)}, u32[]{:S(2)}, u32[]{:S(2)}) %collective-permute-start) | collective-permute-done | bytes 2097184 | tf_op jit(solution)/shard_map/ppermute | solution.py:19
  179.7 0.0 copy-start
  179.7 1.6 collective-permute-done.1.upper_ref
  181.3 0.0 copy-done
  181.3 14.0 %halo_products.1.part_ref = f32[128,128,128]{2,1,0:T(8,128)} custom-call(s32[65]{0:T(128)} %get-tuple-element.10.place_ref, f32[128,128,128]{2,1,0:T(8,128)} %get-tuple-element.11.partial_ref, bf16[65,128,256]{2,1,0:T(8,128)(2,1)} %get-tuple-element.12.left_ref, f32[32,128,128]{2,1,0:T(8,128)} %copy-done, f32[32,128,128]{2,1,0:T(8,128)} %collective-permute-done.1.upper_ref), custom_call_target="tpu_custom_call" | custom-call | tf_op jit(solution)/shard_map/halo_products/pallas_call | solution.py:291
  195.3 79.3 %group_sum.1 = f32[128,128,128]{2,1,0:T(8,128)} custom-call(f32[128,128,128]{2,1,0:T(8,128)} %halo_products.1.part_ref), custom_call_target="tpu_custom_call" | custom-call | flops 2097152 | bytes 16777216 | tf_op jit(solution)/shard_map/group_sum/pallas_call | solution.py:225
  274.7 7.9 %copy.9 = f32[128,128,128]{2,1,0:T(8,128)} copy(f32[128,128,128]{2,1,0:T(8,128)} %group_sum.1) | data formatting | bytes 16777216
Async XLA Ops:
  129.4 50.3 %collective-permute-start = (f32[32,128,128]{2,1,0:T(8,128)}, f32[32,128,128]{2,1,0:T(8,128)S(1)}, u32[]{:S(2)}, u32[]{:S(2)}) collective-permute-start(f32[32,128,128]{2,1,0:T(8,128)} %get-tuple-element.13), channel_id=1, source_target_pairs={{0,1},{1,2},{2,3},{3,4},{4,5},{5,6},{6,7},{7,8},{8,9},{9,10},{10,1... | collective-permute-start | bytes 6291464 | tf_op jit(solution)/shard_map/ppermute | solution.py:19
  133.9 47.4 %collective-permute-start.1 = (f32[32,128,128]{2,1,0:T(8,128)}, f32[32,128,128]{2,1,0:T(8,128)}, u32[]{:S(2)}, u32[]{:S(2)}) collective-permute-start(f32[32,128,128]{2,1,0:T(8,128)} %get-tuple-element.14), channel_id=1, source_target_pairs={{1,0},{2,1},{3,2},{4,3},{5,4},{6,5},{7,6},{8,7},{9,8},{10,9},{11,1... | collective-permute-start | bytes 6291464 | tf_op jit(solution)/shard_map/ppermute | solution.py:19
  179.7 1.7 copy-start

commit v2 on v1

--- a/solution.py
+++ b/solution.py
@@ -11,6 +11,7 @@
 STEP_BLOCKS = 4
 CHUNKS = 8
 VMEM_BYTES = 56 * 1024 * 1024
+SUM_VMEM_BYTES = 44 * 1024 * 1024
 
 
 def shifted(block, axis, distance):
@@ -40,25 +41,14 @@
     return both[:, :width] + both[:, width:]
 
 
-def pick_kernel(send_ref, p_ref, below_ref, above_ref, sem):
-    capacity = send_ref.shape[2]
-
-    def copy(side, j):
-        target = below_ref if side == 0 else above_ref
-        row = jnp.maximum(send_ref[0, side, j], 0)
-        return pltpu.make_async_copy(p_ref.at[row], target.at[j], sem.at[side, j])
-
-    for side in range(2):
-        @pl.loop(0, capacity)
+def pick_kernel(send_ref, p_ref, below_ref, above_ref):
+    for side, target in enumerate((below_ref, above_ref)):
+        @pl.loop(0, target.shape[0])
         def _(j):
-            copy(side, j).start()
-    for side in range(2):
-        @pl.loop(0, capacity)
-        def _(j):
-            copy(side, j).wait()
-
-
-def local_kernel(col_ref, tile_ref, p_ref, a_ref, sum_ref, left_ref, place_ref, right_p):
+            target[j] = p_ref[jnp.maximum(send_ref[0, side, j], 0)]
+
+
+def local_kernel(col_ref, tile_ref, p_ref, a_ref, sum_ref, left_ref, before_ref, last_ref, right_p, place_ref):
     blocks = p_ref.shape[0]
     neighbours = a_ref.shape[1]
     slots = left_ref.shape[0] - 1
@@ -82,8 +72,8 @@
         f = step * STEP_BLOCKS + i
         p_left = left_form(p_ref[f].T)
         for k in range(neighbours):
-            v = col_ref[f, k]
-            t = tile_ref[f, k]
+            v = col_ref[k, f]
+            t = tile_ref[k, f]
             local = v < blocks
             slot = jnp.where(local, slots, v - blocks)
             left = product(p_left, right_form(a_ref[i, k]))
@@ -93,38 +83,40 @@
             triple = product(left_cat, right_p[jnp.minimum(v, blocks - 1)])
             sum_ref[t] += jnp.where(local, triple, 0.0)
 
-
-def halo_kernel(place_ref, partial_ref, left_ref, lower_ref, upper_ref, sum_ref, sem):
-    capacity = lower_ref.shape[0]
-    load = pltpu.make_async_copy(partial_ref, sum_ref, sem)
-    load.start()
-    load.wait()
-    for side, tiles in enumerate((lower_ref, upper_ref)):
-        @pl.loop(0, capacity // 4)
-        def _(group):
-            for i in range(4):
-                j = group * 4 + i
-                place = place_ref[side * capacity + j]
-                triple = product(left_ref[side * capacity + j], right_form(tiles[j]))
-                sum_ref[jnp.maximum(place, 0)] += jnp.where(place >= 0, triple, 0.0)
-
-
-def reduce_kernel(orders, part_ref, out_ref, mine, *rest):
+    @pl.when(step == pl.num_programs(0) - 1)
+    def _():
+        @pl.loop(0, last_ref.shape[0])
+        def _(t):
+            last_ref[t] = slots
+
+        @pl.loop(0, slots)
+        def _(j):
+            t = place_ref[j]
+            before_ref[j] = slots
+
+            @pl.when(t >= 0)
+            def _():
+                before_ref[j] = last_ref[t]
+                last_ref[t] = j
+
+
+def reduce_kernel(orders, before_ref, last_ref, part_ref, left_ref, lower_ref, upper_ref, out_ref, mine, chain, *rest):
     stages = len(orders[0])
     bufs = rest[:stages]
     load_sem, send_sem, recv_sem = rest[stages:]
     me = lax.axis_index("bulk")
     tiles = part_ref.shape[0]
-    chunks = mine.shape[0]
+    chunks = CHUNKS
+    capacity = lower_ref.shape[0]
+    slots = 2 * capacity
     width = tiles // chunks
     ways = len(orders)
     bit = [(me // 2**b) % 2 for b in range(stages)]
     partner = [me + 2**b * (1 - 2 * bit[b]) for b in range(stages)]
 
     def load(c, way):
-        first = orders[way][0]
-        at = c * width + bit[first] * (width // 2)
-        return pltpu.make_async_copy(part_ref.at[pl.ds(at, width // 2)], mine.at[c], load_sem.at[c])
+        here = pl.ds(c * width, width)
+        return pltpu.make_async_copy(part_ref.at[here], mine.at[here], load_sem.at[c])
 
     def keep(c, way, s):
         at = c * width
@@ -138,7 +130,7 @@
         b = orders[way][s]
         size = width >> (s + 1)
         if s == 0:
-            src = part_ref.at[pl.ds(c * width + (1 - bit[b]) * size, size)]
+            src = mine.at[pl.ds(c * width + (1 - bit[b]) * size, size)]
         else:
             src = bufs[s - 1].at[c, pl.ds((1 - bit[b]) * size, size)]
         return pltpu.make_async_remote_copy(
@@ -162,7 +154,7 @@
         @pl.loop(0, size)
         def _(j):
             if s == 0:
-                own = mine[c, j]
+                own = mine[c * width + bit[b] * size + j]
             else:
                 own = bufs[s - 1][c, bit[b] * size + j]
             total = bufs[s][c, j] + own
@@ -181,13 +173,30 @@
     barrier = pltpu.get_barrier_semaphore()
     for b in range(stages):
         pl.semaphore_signal(barrier, inc=1, device_id={"bulk": partner[b]}, device_id_type=pl.DeviceIdType.MESH)
+
+    chain[slots] = jnp.zeros(chain.shape[1:], jnp.float32)
+    for side, tiles_ref in enumerate((lower_ref, upper_ref)):
+        @pl.loop(0, capacity // 4)
+        def _(group):
+            for i in range(4):
+                j = group * 4 + i
+                slot = side * capacity + j
+                triple = product(left_ref[slot], right_form(tiles_ref[j]))
+                chain[slot] = triple + chain[before_ref[slot]]
+
     pl.semaphore_wait(barrier, stages)
 
-    each(lambda c, way: scatter(c, way, 0).start())
+    def finish(c, way):
+        load(c, way).wait()
+
+        @pl.loop(0, width)
+        def _(i):
+            t = c * width + i
+            mine[t] += chain[last_ref[t]]
+        scatter(c, way, 0).start()
+    each(finish)
     for s in range(stages):
         def reduce_step(c, way, s=s):
-            if s == 0:
-                load(c, way).wait()
             scatter(c, way, s).wait_recv()
             add(c, way, s)
             if s + 1 < stages:
@@ -209,7 +218,7 @@
     each(drain)
 
 
-def group_sum(partial):
+def group_sum(before, last, partial, left, lower, upper):
     devices = lax.axis_size("bulk")
     stages = devices.bit_length() - 1
     tiles, rows, columns = partial.shape
@@ -221,13 +230,15 @@
     else:
         orders = (bits, bits[stages // 2:] + bits[:stages // 2])
     tile = (rows, columns)
+    smem_spec = pl.BlockSpec(memory_space=pltpu.SMEM)
+    vmem_spec = pl.BlockSpec(memory_space=pltpu.VMEM)
     vmem = functools.partial(pltpu.VMEM, dtype=jnp.float32)
     return pl.pallas_call(
         functools.partial(reduce_kernel, orders),
-        out_shape=jax.ShapeDtypeStruct(partial.shape, jnp.float32),
-        in_specs=[pl.BlockSpec(memory_space=pl.ANY)],
-        out_specs=pl.BlockSpec(memory_space=pltpu.VMEM),
-        scratch_shapes=[vmem((CHUNKS, width // 2) + tile)]
+        out_shape=pltpu.VMEM(partial.shape, jnp.float32),
+        in_specs=[smem_spec, smem_spec, pl.BlockSpec(memory_space=pl.ANY), vmem_spec, vmem_spec, vmem_spec],
+        out_specs=vmem_spec,
+        scratch_shapes=[vmem(partial.shape), vmem((2 * lower.shape[0] + 1,) + tile)]
         + [vmem((CHUNKS, width >> (s + 1)) + tile) for s in range(stages)]
         + [
             pltpu.SemaphoreType.DMA((CHUNKS,)),
@@ -235,10 +246,10 @@
             pltpu.SemaphoreType.DMA((2 * stages, CHUNKS)),
         ],
         compiler_params=pltpu.CompilerParams(
-            collective_id=0, has_side_effects=True, vmem_limit_bytes=VMEM_BYTES),
+            collective_id=0, has_side_effects=True, vmem_limit_bytes=SUM_VMEM_BYTES),
         cost_estimate=pl.CostEstimate(flops=tiles * rows * columns, bytes_accessed=8 * tiles * rows * columns, transcendentals=0),
         name="group_sum",
-    )(partial)
+    )(before, last, partial, left, lower, upper)
 
 
 def shards(p_tiles, a_tiles, col_ref, send_list, coarse_tile):
@@ -247,7 +258,6 @@
     capacity = send_list.shape[2]
     slots = 2 * capacity
     tile = (rows, columns)
-    any_spec = pl.BlockSpec(memory_space=pl.ANY)
     smem_spec = pl.BlockSpec(memory_space=pltpu.SMEM)
     vmem_spec = pl.BlockSpec(memory_space=pltpu.VMEM)
 
@@ -255,9 +265,8 @@
     to_below, to_above = pl.pallas_call(
         pick_kernel,
         out_shape=(sent, sent),
-        in_specs=[smem_spec, any_spec],
-        out_specs=(any_spec, any_spec),
-        scratch_shapes=[pltpu.SemaphoreType.DMA((2, capacity))],
+        in_specs=[smem_spec, vmem_spec],
+        out_specs=(vmem_spec, vmem_spec),
         name="pick",
     )(send_list, p_tiles)
     lower = shifted(to_above, ("group", "bulk"), 1)
@@ -265,12 +274,13 @@
 
     couplings = blocks * neighbours
     whole = lambda *shape: pl.BlockSpec(shape, lambda s, *_: (0,) * len(shape))
-    partial, left, place = pl.pallas_call(
+    partial, left, before, last = pl.pallas_call(
         local_kernel,
         out_shape=(
             jax.ShapeDtypeStruct((CT,) + tile, jnp.float32),
             jax.ShapeDtypeStruct((slots + 1, rows, 2 * columns), jnp.bfloat16),
-            jax.ShapeDtypeStruct((slots + 1,), jnp.int32),
+            jax.ShapeDtypeStruct((slots,), jnp.int32),
+            jax.ShapeDtypeStruct((CT,), jnp.int32),
         ),
         grid_spec=pltpu.PrefetchScalarGridSpec(
             num_scalar_prefetch=2,
@@ -279,25 +289,16 @@
                 whole(blocks, *tile),
                 pl.BlockSpec((STEP_BLOCKS, neighbours) + tile, lambda s, *_: (s, 0, 0, 0)),
             ],
-            out_specs=(whole(CT, *tile), whole(slots + 1, rows, 2 * columns), pl.BlockSpec(memory_space=pltpu.SMEM)),
-            scratch_shapes=[pltpu.VMEM((blocks, 2 * rows, 2 * columns), jnp.bfloat16)],
+            out_specs=(whole(CT, *tile), whole(slots + 1, rows, 2 * columns), smem_spec, smem_spec),
+            scratch_shapes=[pltpu.VMEM((blocks, 2 * rows, 2 * columns), jnp.bfloat16), pltpu.SMEM((slots + 1,), jnp.int32)],
         ),
         compiler_params=pltpu.CompilerParams(vmem_limit_bytes=VMEM_BYTES),
         cost_estimate=pl.CostEstimate(
             flops=couplings * 16 * rows * rows * columns, bytes_accessed=4 * couplings * rows * columns, transcendentals=0),
         name="local_products",
-    )(col_ref, coarse_tile, p_tiles, a_tiles)
-
-    total = pl.pallas_call(
-        halo_kernel,
-        out_shape=jax.ShapeDtypeStruct((CT,) + tile, jnp.float32),
-        in_specs=[smem_spec, any_spec, vmem_spec, vmem_spec, vmem_spec],
-        out_specs=vmem_spec,
-        scratch_shapes=[pltpu.SemaphoreType.DMA],
-        compiler_params=pltpu.CompilerParams(vmem_limit_bytes=VMEM_BYTES),
-        name="halo_products",
-    )(place, partial, left, lower, upper)
-    return group_sum(total)
+    )(col_ref.T, coarse_tile.T, p_tiles, a_tiles)
+
+    return group_sum(before, last, partial, left, lower, upper)
 
 
 def solution(mesh):

time: 283 us -> 146 us (0.52)
  Pallas kernels: 250 us -> 116 us
  local copies, waits for them, and re-layouts: 10.7 us -> 6 us
    pallas_call x1, Pallas kernels: 129 us -> 4.6 us  [shards(): pl.pallas_call(pick_kernel, out_shape=(sent, sent), in_specs=[smem_spec,...]
    pallas_call x2 -> x1, Pallas kernels: 93.3 us -> 83 us  [group_sum(): pl.pallas_call(functools.partial(reduce_kernel, orders), out_shape=pltpu....]
    unnamed x5 -> x9, local copies, waits for them, and re-layouts: 10.7 us -> 6 us
  transfers between devices with their start and end apart: 2 -> 2, of which waited for: 2 -> 2; matrix products, arithmetic and copies ran while one was open for 1% -> 0% of each run, Pallas kernels for 10% -> 19%
where the time goes in v2:
time: 146 us; the launch traced here: 145 us
  Pallas kernels  116 us (79%)
  waiting for transfers between devices  17.2 us (12%)
  starting transfers between devices  6.42 us (4%)
  local copies, waits for them, and re-layouts  6 us (4%)
    pallas_call x1, Pallas kernels, group_sum(): pl.pallas_call(functools.partial(reduce_kernel, orders), out_shape=pltpu....  83 us
    pallas_call x1, Pallas kernels, shards(): pl.pallas_call(local_kernel, out_shape=(jax.ShapeDtypeStruct((CT,) + tile...  28.2 us
    ppermute x2, waiting for transfers between devices, shifted(): return lax.ppermute(block, axis, route)  17.2 us
    ppermute x2, starting transfers between devices, shifted(): return lax.ppermute(block, axis, route)  6.42 us
    unnamed x9, local copies, waits for them, and re-layouts  6 us
    pallas_call x1, Pallas kernels, shards(): pl.pallas_call(pick_kernel, out_shape=(sent, sent), in_specs=[smem_spec,...  4.6 us
  transfers between devices with their start and end apart: 2, of which 2 were waited for; matrix products, arithmetic and copies ran while one was open for 0% of the time, Pallas kernels for 19%

profile of v2, /device:TPU:1, one launch (start us, length us, event | category | flops | bytes accessed | tf_op | source)
XLA Modules:
  0.0 145.4 jit_solution(14330328333045622069)
XLA Ops:
  0.0 4.6 %pick.1 = (f32[32,128,128]{2,1,0:T(8,128)}, f32[32,128,128]{2,1,0:T(8,128)}) custom-call(s32[1,2,32]{2,1,0:T(2,128)} %send_ref.1, f32[48,128,128]{2,1,0:T(8,128)} %p_ref.3), custom_call_target="tpu_custom_call" | custom-call | tf_op jit(solution)/shard_map/pick/pallas_call | solution.py:265
  4.6 4.5 %collective-permute-start = (f32[32,128,128]{2,1,0:T(8,128)}, f32[32,128,128]{2,1,0:T(8,128)S(1)}, u32[]{:S(2)}, u32[]{:S(2)}) collective-permute-start(f32[32,128,128]{2,1,0:T(8,128)} %get-tuple-element.15), channel_id=1, source_target_pairs={{0,1},{1,2},{2,3},{3,4},{4,5},{5,6},{6,7},{7,8},{8,9},{9,10},{10,1... | collective-permute-start | bytes 6291464 | tf_op jit(solution)/shard_map/ppermute | solution.py:20
  9.1 1.9 %collective-permute-start.1 = (f32[32,128,128]{2,1,0:T(8,128)}, f32[32,128,128]{2,1,0:T(8,128)S(1)}, u32[]{:S(2)}, u32[]{:S(2)}) collective-permute-start(f32[32,128,128]{2,1,0:T(8,128)} %get-tuple-element.16), channel_id=1, source_target_pairs={{1,0},{2,1},{3,2},{4,3},{5,4},{6,5},{7,6},{8,7},{9,8},{10,9},{11,1... | collective-permute-start | bytes 6291464 | tf_op jit(solution)/shard_map/ppermute | solution.py:20
  11.0 28.2 %local_products.1 = (f32[128,128,128]{2,1,0:T(8,128)}, bf16[65,128,256]{2,1,0:T(8,128)(2,1)}, s32[64]{0:T(128)}, s32[128]{0:T(128)}) custom-call(s32[7,48]{1,0:T(8,128)} %bitcast.2, s32[7,48]{1,0:T(8,128)} %bitcast.3, f32[48,128,128]{2,1,0:T(8,128)} %p_ref.3, f32[48,7,128,128]{3,2,1,0:T(8,128)} %a_ref.1), custom_call_target="tpu_custom_call" | custom-call | flops 11274289152 | bytes 22020096 | tf_op jit(solution)/shard_map/local_products/pallas_call | solution.py:277
  39.2 15.6 %collective-permute-done.lower_ref = f32[32,128,128]{2,1,0:T(8,128)S(1)} collective-permute-done((f32[32,128,128]{2,1,0:T(8,128)}, f32[32,128,128]{2,1,0:T(8,128)S(1)}, u32[]{:S(2)}, u32[]{:S(2)}) %collective-permute-start) | collective-permute-done | bytes 2097184 | tf_op jit(solution)/shard_map/ppermute | solution.py:20
  54.8 0.0 copy-start.2
  54.8 1.5 %collective-permute-done.1.upper_ref = f32[32,128,128]{2,1,0:T(8,128)S(1)} collective-permute-done((f32[32,128,128]{2,1,0:T(8,128)}, f32[32,128,128]{2,1,0:T(8,128)S(1)}, u32[]{:S(2)}, u32[]{:S(2)}) %collective-permute-start.1) | collective-permute-done | bytes 2097184 | tf_op jit(solution)/shard_map/ppermute | solution.py:20
  56.4 0.0 copy-start.3
  56.4 0.0 copy-done.2
  56.4 1.3 copy-done.3
  57.7 0.0 copy-start
  57.7 0.6 copy-done
  58.3 0.0 copy-start.1
  58.3 0.7 copy-done.1
  59.0 83.0 %group_sum.1 = f32[128,128,128]{2,1,0:T(8,128)S(1)} custom-call(s32[64]{0:T(128)S(1)} %copy-done, s32[128]{0:T(128)S(1)} %copy-done.1, f32[128,128,128]{2,1,0:T(8,128)} %get-tuple-element.13.part_ref, bf16[65,128,256]{2,1,0:T(8,128)(2,1)} %get-tuple-element.14.left_ref, f32[32,128,128]{2,1,0:T(8,128)} %copy-done.2, f32[32,128,128]{2,1,0:T(8,128)} %copy-done.3), custom_call_target="tpu_custom_call" | custom-call | flops 2097152 | bytes 16777216 | tf_op jit(solution)/shard_map/group_sum/pallas_call | solution.py:236
  142.0 3.4 %copy.7 = f32[128,128,128]{2,1,0:T(8,128)} copy(f32[128,128,128]{2,1,0:T(8,128)S(1)} %group_sum.1) | data formatting | bytes 16777216
Async XLA Ops:
  4.6 50.2 %collective-permute-start = (f32[32,128,128]{2,1,0:T(8,128)}, f32[32,128,128]{2,1,0:T(8,128)S(1)}, u32[]{:S(2)}, u32[]{:S(2)}) collective-permute-start(f32[32,128,128]{2,1,0:T(8,128)} %get-tuple-element.15), channel_id=1, source_target_pairs={{0,1},{1,2},{2,3},{3,4},{4,5},{5,6},{6,7},{7,8},{8,9},{9,10},{10,1... | collective-permute-start | bytes 6291464 | tf_op jit(solution)/shard_map/ppermute | solution.py:20
  9.1 47.3 %collective-permute-start.1 = (f32[32,128,128]{2,1,0:T(8,128)}, f32[32,128,128]{2,1,0:T(8,128)S(1)}, u32[]{:S(2)}, u32[]{:S(2)}) collective-permute-start(f32[32,128,128]{2,1,0:T(8,128)} %get-tuple-element.16), channel_id=1, source_target_pairs={{1,0},{2,1},{3,2},{4,3},{5,4},{6,5},{7,6},{8,7},{9,8},{10,9},{11,1... | collective-permute-start | bytes 6291464 | tf_op jit(solution)/shard_map/ppermute | solution.py:20
  54.8 1.5 %copy-start.2 = (f32[32,128,128]{2,1,0:T(8,128)}, f32[32,128,128]{2,1,0:T(8,128)S(1)}, u32[]{:S(2)}) copy-start(f32[32,128,128]{2,1,0:T(8,128)S(1)} %collective-permute-done.lower_ref) | copy-start | bytes 6291460
  56.4 1.3 copy-start.3
  57.7 0.6 copy-start
  58.3 0.7 copy-start.1

commit v3 on v2

--- a/solution.py
+++ b/solution.py
@@ -9,8 +9,9 @@
 
 CT = 128
 STEP_BLOCKS = 4
-CHUNKS = 8
-VMEM_BYTES = 56 * 1024 * 1024
+CHUNKS = 16
+PIECE = 8
+VMEM_BYTES = 52 * 1024 * 1024
 SUM_VMEM_BYTES = 44 * 1024 * 1024
 
 
@@ -41,14 +42,23 @@
     return both[:, :width] + both[:, width:]
 
 
-def pick_kernel(send_ref, p_ref, below_ref, above_ref):
-    for side, target in enumerate((below_ref, above_ref)):
+def pick_kernel(send_ref, p_ref, below_ref, above_ref, sem):
+    def copy(side, target, j):
+        row = jnp.maximum(send_ref[0, side, j], 0)
+        return pltpu.make_async_copy(p_ref.at[row], target.at[j], sem.at[side, j])
+
+    targets = ((1, above_ref), (0, below_ref))
+    for side, target in targets:
         @pl.loop(0, target.shape[0])
         def _(j):
-            target[j] = p_ref[jnp.maximum(send_ref[0, side, j], 0)]
-
-
-def local_kernel(col_ref, tile_ref, p_ref, a_ref, sum_ref, left_ref, before_ref, last_ref, right_p, place_ref):
+            copy(side, target, j).start()
+    for side, target in targets:
+        @pl.loop(0, target.shape[0])
+        def _(j):
+            copy(side, target, j).wait()
+
+
+def local_kernel(col_ref, tile_ref, p_ref, a_ref, sum_ref, left_ref, link_ref, right_p, place_ref):
     blocks = p_ref.shape[0]
     neighbours = a_ref.shape[1]
     slots = left_ref.shape[0] - 1
@@ -85,29 +95,45 @@
 
     @pl.when(step == pl.num_programs(0) - 1)
     def _():
-        @pl.loop(0, last_ref.shape[0])
+        @pl.loop(0, sum_ref.shape[0])
         def _(t):
-            last_ref[t] = slots
+            link_ref[slots + t] = slots
 
         @pl.loop(0, slots)
         def _(j):
             t = place_ref[j]
-            before_ref[j] = slots
+            link_ref[j] = slots
 
             @pl.when(t >= 0)
             def _():
-                before_ref[j] = last_ref[t]
-                last_ref[t] = j
-
-
-def reduce_kernel(orders, before_ref, last_ref, part_ref, left_ref, lower_ref, upper_ref, out_ref, mine, chain, *rest):
+                link_ref[j] = link_ref[slots + t]
+                link_ref[slots + t] = j
+
+
+def lower_kernel(link_ref, left_ref, lower_ref, chain_ref):
+    group = lower_ref.shape[0]
+    capacity = chain_ref.shape[0] - 1
+    step = pl.program_id(0)
+
+    @pl.when(step == 0)
+    def _():
+        chain_ref[capacity] = jnp.zeros(chain_ref.shape[1:], jnp.float32)
+
+    for i in range(group):
+        slot = step * group + i
+        triple = product(left_ref[i], right_form(lower_ref[i]))
+        chain_ref[slot] = triple + chain_ref[jnp.minimum(link_ref[slot], capacity)]
+
+
+def reduce_kernel(orders, link_hbm, part_ref, left_hbm, lower_hbm, upper, out_ref, link_ref, left, mine, chain, *rest):
     stages = len(orders[0])
     bufs = rest[:stages]
-    load_sem, send_sem, recv_sem = rest[stages:]
+    load_sem, halo_sem, send_sem, recv_sem = rest[stages:]
     me = lax.axis_index("bulk")
     tiles = part_ref.shape[0]
-    chunks = CHUNKS
-    capacity = lower_ref.shape[0]
+    chunks = load_sem.shape[0]
+    capacity = upper.shape[0]
+    pieces = capacity // PIECE
     slots = 2 * capacity
     width = tiles // chunks
     ways = len(orders)
@@ -169,20 +195,34 @@
             for way in range(ways):
                 body(g * ways + way, way)
 
+    link_load = pltpu.make_async_copy(link_hbm, link_ref, halo_sem.at[pieces])
+    lower_load = pltpu.make_async_copy(
+        lower_hbm.at[pl.ds(0, capacity)], chain.at[pl.ds(0, capacity)], halo_sem.at[pieces + 1])
+
+    def left_load(g):
+        return pltpu.make_async_copy(
+            left_hbm.at[pl.ds(capacity + g * PIECE, PIECE)], left.at[pl.ds(g * PIECE, PIECE)], halo_sem.at[g])
+
+    link_load.start()
+    for g in range(pieces):
+        left_load(g).start()
+    lower_load.start()
     each(lambda c, way: load(c, way).start())
     barrier = pltpu.get_barrier_semaphore()
     for b in range(stages):
         pl.semaphore_signal(barrier, inc=1, device_id={"bulk": partner[b]}, device_id_type=pl.DeviceIdType.MESH)
 
     chain[slots] = jnp.zeros(chain.shape[1:], jnp.float32)
-    for side, tiles_ref in enumerate((lower_ref, upper_ref)):
-        @pl.loop(0, capacity // 4)
-        def _(group):
-            for i in range(4):
-                j = group * 4 + i
-                slot = side * capacity + j
-                triple = product(left_ref[slot], right_form(tiles_ref[j]))
-                chain[slot] = triple + chain[before_ref[slot]]
+    link_load.wait()
+    lower_load.wait()
+
+    @pl.loop(0, pieces)
+    def _(g):
+        left_load(g).wait()
+        for i in range(PIECE):
+            j = g * PIECE + i
+            triple = product(left[j], right_form(upper[j]))
+            chain[capacity + j] = triple + chain[link_ref[capacity + j]]
 
     pl.semaphore_wait(barrier, stages)
 
@@ -192,7 +232,7 @@
         @pl.loop(0, width)
         def _(i):
             t = c * width + i
-            mine[t] += chain[last_ref[t]]
+            mine[t] += chain[link_ref[slots + t]]
         scatter(c, way, 0).start()
     each(finish)
     for s in range(stages):
@@ -218,11 +258,13 @@
     each(drain)
 
 
-def group_sum(before, last, partial, left, lower, upper):
+def group_sum(links, partial, left, lower, upper):
     devices = lax.axis_size("bulk")
     stages = devices.bit_length() - 1
     tiles, rows, columns = partial.shape
-    width = tiles // CHUNKS
+    chunks = min(CHUNKS, tiles // devices)
+    width = tiles // chunks
+    capacity = upper.shape[0]
     bits = tuple(range(stages))
     if stages % 2:
         half = (stages - 1) // 2
@@ -230,26 +272,31 @@
     else:
         orders = (bits, bits[stages // 2:] + bits[:stages // 2])
     tile = (rows, columns)
-    smem_spec = pl.BlockSpec(memory_space=pltpu.SMEM)
-    vmem_spec = pl.BlockSpec(memory_space=pltpu.VMEM)
+    hbm_spec = pl.BlockSpec(memory_space=pltpu.HBM)
     vmem = functools.partial(pltpu.VMEM, dtype=jnp.float32)
     return pl.pallas_call(
         functools.partial(reduce_kernel, orders),
         out_shape=pltpu.VMEM(partial.shape, jnp.float32),
-        in_specs=[smem_spec, smem_spec, pl.BlockSpec(memory_space=pl.ANY), vmem_spec, vmem_spec, vmem_spec],
-        out_specs=vmem_spec,
-        scratch_shapes=[vmem(partial.shape), vmem((2 * lower.shape[0] + 1,) + tile)]
-        + [vmem((CHUNKS, width >> (s + 1)) + tile) for s in range(stages)]
+        in_specs=[hbm_spec] * 4 + [pl.BlockSpec(memory_space=pltpu.VMEM)],
+        out_specs=pl.BlockSpec(memory_space=pltpu.VMEM),
+        scratch_shapes=[
+            pltpu.SMEM(links.shape, jnp.int32),
+            pltpu.VMEM((capacity,) + left.shape[1:], left.dtype),
+            vmem(partial.shape),
+            vmem((2 * capacity + 1,) + tile),
+        ]
+        + [vmem((chunks, width >> (s + 1)) + tile) for s in range(stages)]
         + [
-            pltpu.SemaphoreType.DMA((CHUNKS,)),
-            pltpu.SemaphoreType.DMA((2 * stages, CHUNKS)),
-            pltpu.SemaphoreType.DMA((2 * stages, CHUNKS)),
+            pltpu.SemaphoreType.DMA((chunks,)),
+            pltpu.SemaphoreType.DMA((capacity // PIECE + 2,)),
+            pltpu.SemaphoreType.DMA((2 * stages, chunks)),
+            pltpu.SemaphoreType.DMA((2 * stages, chunks)),
         ],
         compiler_params=pltpu.CompilerParams(
             collective_id=0, has_side_effects=True, vmem_limit_bytes=SUM_VMEM_BYTES),
         cost_estimate=pl.CostEstimate(flops=tiles * rows * columns, bytes_accessed=8 * tiles * rows * columns, transcendentals=0),
         name="group_sum",
-    )(before, last, partial, left, lower, upper)
+    )(links, partial, left, lower, upper)
 
 
 def shards(p_tiles, a_tiles, col_ref, send_list, coarse_tile):
@@ -260,27 +307,29 @@
     tile = (rows, columns)
     smem_spec = pl.BlockSpec(memory_space=pltpu.SMEM)
     vmem_spec = pl.BlockSpec(memory_space=pltpu.VMEM)
-
-    sent = jax.ShapeDtypeStruct((capacity,) + tile, jnp.float32)
+    hbm_spec = pl.BlockSpec(memory_space=pltpu.HBM)
+
+    sent = pltpu.VMEM((capacity,) + tile, jnp.float32)
     to_below, to_above = pl.pallas_call(
         pick_kernel,
         out_shape=(sent, sent),
-        in_specs=[smem_spec, vmem_spec],
+        in_specs=[smem_spec, hbm_spec],
         out_specs=(vmem_spec, vmem_spec),
+        scratch_shapes=[pltpu.SemaphoreType.DMA((2, capacity))],
+        compiler_params=pltpu.CompilerParams(vmem_limit_bytes=8 * 1024 * 1024),
         name="pick",
-    )(send_list, p_tiles)
+    )(send_list, pltpu.with_memory_space_constraint(p_tiles, pltpu.HBM))
     lower = shifted(to_above, ("group", "bulk"), 1)
     upper = shifted(to_below, ("group", "bulk"), -1)
 
     couplings = blocks * neighbours
     whole = lambda *shape: pl.BlockSpec(shape, lambda s, *_: (0,) * len(shape))
-    partial, left, before, last = pl.pallas_call(
+    partial, left, links = pl.pallas_call(
         local_kernel,
         out_shape=(
             jax.ShapeDtypeStruct((CT,) + tile, jnp.float32),
             jax.ShapeDtypeStruct((slots + 1, rows, 2 * columns), jnp.bfloat16),
-            jax.ShapeDtypeStruct((slots,), jnp.int32),
-            jax.ShapeDtypeStruct((CT,), jnp.int32),
+            jax.ShapeDtypeStruct((-(-(slots + CT) // 128) * 128,), jnp.int32),
         ),
         grid_spec=pltpu.PrefetchScalarGridSpec(
             num_scalar_prefetch=2,
@@ -289,7 +338,7 @@
                 whole(blocks, *tile),
                 pl.BlockSpec((STEP_BLOCKS, neighbours) + tile, lambda s, *_: (s, 0, 0, 0)),
             ],
-            out_specs=(whole(CT, *tile), whole(slots + 1, rows, 2 * columns), smem_spec, smem_spec),
+            out_specs=(whole(CT, *tile), whole(slots + 1, rows, 2 * columns), smem_spec),
             scratch_shapes=[pltpu.VMEM((blocks, 2 * rows, 2 * columns), jnp.bfloat16), pltpu.SMEM((slots + 1,), jnp.int32)],
         ),
         compiler_params=pltpu.CompilerParams(vmem_limit_bytes=VMEM_BYTES),
@@ -298,7 +347,24 @@
         name="local_products",
     )(col_ref.T, coarse_tile.T, p_tiles, a_tiles)
 
-    return group_sum(before, last, partial, left, lower, upper)
+    lower_chain = pl.pallas_call(
+        lower_kernel,
+        out_shape=pltpu.HBM((capacity + 1,) + tile, jnp.float32),
+        grid_spec=pltpu.PrefetchScalarGridSpec(
+            num_scalar_prefetch=1,
+            grid=(capacity // PIECE,),
+            in_specs=[
+                pl.BlockSpec((PIECE, rows, 2 * columns), lambda s, *_: (s, 0, 0)),
+                pl.BlockSpec((PIECE,) + tile, lambda s, *_: (s, 0, 0)),
+            ],
+            out_specs=whole(capacity + 1, *tile),
+        ),
+        compiler_params=pltpu.CompilerParams(vmem_limit_bytes=24 * 1024 * 1024),
+        cost_estimate=pl.CostEstimate(
+            flops=capacity * 8 * rows * rows * columns, bytes_accessed=12 * capacity * rows * columns, transcendentals=0),
+        name="lower_products",
+    )(links, left, lower)
+    return group_sum(links, partial, left, lower_chain, pltpu.with_memory_space_constraint(upper, pltpu.VMEM))
 
 
 def solution(mesh):

time: 146 us -> 144 us (0.986)
  waiting for transfers between devices: 17.2 us -> 15.2 us
    pallas_call x0 -> x1, Pallas kernels: none -> 3.25 us  [shards(): pl.pallas_call(lower_kernel, out_shape=pltpu.HBM((capacity + 1,) + tile,...]
    pallas_call x1, Pallas kernels: 83 us -> 79.8 us  [group_sum(): pl.pallas_call(functools.partial(reduce_kernel, orders), out_shape=pltpu....]
    ppermute x2, waiting for transfers between devices: 17.2 us -> 15.2 us  [shifted(): return lax.ppermute(block, axis, route)]
    unnamed x9 -> x11, local copies, waits for them, and re-layouts: 6 us -> 6.3 us
  transfers between devices with their start and end apart: 2 -> 2, of which waited for: 2 -> 1; matrix products, arithmetic and copies ran while one was open for 0% -> 0% of each run, Pallas kernels for 19% -> 22%
where the time goes in v3:
time: 144 us; the launch traced here: 143 us
  Pallas kernels  116 us (81%)
  waiting for transfers between devices  15.2 us (11%)
  local copies, waits for them, and re-layouts  6.3 us (4%)
  starting transfers between devices  5.44 us (4%)
    pallas_call x1, Pallas kernels, group_sum(): pl.pallas_call(functools.partial(reduce_kernel, orders), out_shape=pltpu....  79.8 us
    pallas_call x1, Pallas kernels, shards(): pl.pallas_call(local_kernel, out_shape=(jax.ShapeDtypeStruct((CT,) + tile...  28.2 us
    ppermute x2, waiting for transfers between devices, shifted(): return lax.ppermute(block, axis, route)  15.2 us
    unnamed x11, local copies, waits for them, and re-layouts  6.3 us
    ppermute x2, starting transfers between devices, shifted(): return lax.ppermute(block, axis, route)  5.44 us
    pallas_call x1, Pallas kernels, shards(): pl.pallas_call(pick_kernel, out_shape=(sent, sent), in_specs=[smem_spec,...  4.38 us
    pallas_call x1, Pallas kernels, shards(): pl.pallas_call(lower_kernel, out_shape=pltpu.HBM((capacity + 1,) + tile,...  3.25 us
  transfers between devices with their start and end apart: 2, of which 1 were waited for; matrix products, arithmetic and copies ran while one was open for 0% of the time, Pallas kernels for 22%

profile of v3, /device:TPU:1, one launch (start us, length us, event | category | flops | bytes accessed | tf_op | source)
XLA Modules:
  0.0 142.7 jit_solution(12948808877431933790)
XLA Ops:
  0.0 0.0 copy-start.2
  0.0 0.7 copy-done.2
  0.7 0.0 copy-start.3
  0.7 0.0 copy-start.4
  0.7 4.4 %pick.1 = (f32[32,128,128]{2,1,0:T(8,128)S(1)}, f32[32,128,128]{2,1,0:T(8,128)S(1)}) custom-call(s32[1,2,32]{2,1,0:T(2,128)S(1)} %copy-done.2, f32[48,128,128]{2,1,0:T(8,128)} %p_ref.3), custom_call_target="tpu_custom_call" | custom-call | tf_op jit(solution)/shard_map/pick/pallas_call | solution.py:313
  5.1 3.5 %collective-permute-start = (f32[32,128,128]{2,1,0:T(8,128)S(1)}, f32[32,128,128]{2,1,0:T(8,128)S(1)}, u32[]{:S(2)}, u32[]{:S(2)}) collective-permute-start(f32[32,128,128]{2,1,0:T(8,128)S(1)} %get-tuple-element.13), channel_id=1, source_target_pairs={{0,1},{1,2},{2,3},{3,4},{4,5},{5,6},{6,7},{7,8},{8,9},{9,10},{10,1... | collective-permute-start | bytes 6291464 | tf_op jit(solution)/shard_map/ppermute | solution.py:21
  8.6 1.9 %collective-permute-start.1 = (f32[32,128,128]{2,1,0:T(8,128)S(1)}, f32[32,128,128]{2,1,0:T(8,128)S(1)}, u32[]{:S(2)}, u32[]{:S(2)}) collective-permute-start(f32[32,128,128]{2,1,0:T(8,128)S(1)} %get-tuple-element.14), channel_id=1, source_target_pairs={{1,0},{2,1},{3,2},{4,3},{5,4},{6,5},{7,6},{8,7},{9,8},{10,9},{11,1... | collective-permute-start | bytes 6291464 | tf_op jit(solution)/shard_map/ppermute | solution.py:21
  10.5 0.0 copy-done.3
  10.5 0.0 copy-done.4
  10.6 28.2 %local_products.1 = (f32[128,128,128]{2,1,0:T(8,128)}, bf16[65,128,256]{2,1,0:T(8,128)(2,1)}, s32[256]{0:T(256)S(1)}) custom-call(s32[7,48]{1,0:T(8,128)S(1)} %bitcast.2, s32[7,48]{1,0:T(8,128)S(1)} %bitcast.3, f32[48,128,128]{2,1,0:T(8,128)} %p_ref.3, f32[48,7,128,128]{3,2,1,0:T(8,128)} %a_ref.1), custom_call_target="tpu_custom_call" | custom-call | flops 11274289152 | bytes 22020096 | tf_op jit(solution)/shard_map/local_products/pallas_call | solution.py:327
  38.8 0.0 copy-start.1
  38.8 15.2 %collective-permute-done.lower_ref = f32[32,128,128]{2,1,0:T(8,128)S(1)} collective-permute-done((f32[32,128,128]{2,1,0:T(8,128)S(1)}, f32[32,128,128]{2,1,0:T(8,128)S(1)}, u32[]{:S(2)}, u32[]{:S(2)}) %collective-permute-start) | collective-permute-done | bytes 2097184 | tf_op jit(solution)/shard_map/ppermute | solution.py:21
  54.0 0.0 copy-start
  54.0 2.2 %copy-done = bf16[65,128,256]{2,1,0:T(8,128)(2,1)S(1)} copy-done((bf16[65,128,256]{2,1,0:T(8,128)(2,1)S(1)}, bf16[65,128,256]{2,1,0:T(8,128)(2,1)}, u32[]{:S(2)}) %copy-start) | copy-done | bytes 4259864
  56.2 3.2 %lower_products.1.lower_hbm = f32[33,128,128]{2,1,0:T(8,128)} custom-call(s32[256]{0:T(256)S(1)} %get-tuple-element.10.link_ref.link_hbm, bf16[65,128,256]{2,1,0:T(8,128)(2,1)S(1)} %copy-done, f32[32,128,128]{2,1,0:T(8,128)S(1)} %collective-permute-done.lower_ref), custom_call_target="tpu_custom_call" | custom-call | flops 536870912 | bytes 6291456 | tf_op jit(solution)/shard_map/lower_products/pallas_call | solution.py:350
  59.5 0.0 copy-done.1
  59.5 0.0 collective-permute-done.1.upper
  59.5 79.8 %group_sum.1 = f32[128,128,128]{2,1,0:T(8,128)S(1)} custom-call(s32[256]{0:T(256)} %copy-done.1, f32[128,128,128]{2,1,0:T(8,128)} %get-tuple-element.11.part_ref, bf16[65,128,256]{2,1,0:T(8,128)(2,1)} %get-tuple-element.12.left_ref.left_hbm, f32[33,128,128]{2,1,0:T(8,128)} %lower_products.1.lower_hbm, f32[32,128,128]{2,1,0:T(8,128)S(1)} %collective-permute-done.1.upper), custom_call_target="tpu_custom_call" | custom-call | flops 2097152 | bytes 16777216 | tf_op jit(solution)/shard_map/group_sum/pallas_call | solution.py:277
  139.3 3.4 %copy.7 = f32[128,128,128]{2,1,0:T(8,128)} copy(f32[128,128,128]{2,1,0:T(8,128)S(1)} %group_sum.1) | data formatting | bytes 16777216
Async XLA Ops:
  0.0 0.7 copy-start.2
  0.7 9.9 %copy-start.3 = (s32[48,7]{0,1:T(8,128)S(1)}, s32[48,7]{0,1:T(8,128)}, u32[]{:S(2)}) copy-start(s32[48,7]{0,1:T(8,128)} %param.7) | copy-start | bytes 4036
  0.7 9.9 %copy-start.4 = (s32[48,7]{0,1:T(8,128)S(1)}, s32[48,7]{0,1:T(8,128)}, u32[]{:S(2)}) copy-start(s32[48,7]{0,1:T(8,128)} %param.9) | copy-start | bytes 4036
  5.1 49.0 %collective-permute-start = (f32[32,128,128]{2,1,0:T(8,128)S(1)}, f32[32,128,128]{2,1,0:T(8,128)S(1)}, u32[]{:S(2)}, u32[]{:S(2)}) collective-permute-start(f32[32,128,128]{2,1,0:T(8,128)S(1)} %get-tuple-element.13), channel_id=1, source_target_pairs={{0,1},{1,2},{2,3},{3,4},{4,5},{5,6},{6,7},{7,8},{8,9},{9,10},{10,1... | collective-permute-start | bytes 6291464 | tf_op jit(solution)/shard_map/ppermute | solution.py:21
  8.6 50.9 %collective-permute-start.1 = (f32[32,128,128]{2,1,0:T(8,128)S(1)}, f32[32,128,128]{2,1,0:T(8,128)S(1)}, u32[]{:S(2)}, u32[]{:S(2)}) collective-permute-start(f32[32,128,128]{2,1,0:T(8,128)S(1)} %get-tuple-element.14), channel_id=1, source_target_pairs={{1,0},{2,1},{3,2},{4,3},{5,4},{6,5},{7,6},{8,7},{9,8},{10,9},{11,1... | collective-permute-start | bytes 6291464 | tf_op jit(solution)/shard_map/ppermute | solution.py:21
  38.8 20.7 %copy-start.1 = (s32[256]{0:T(256)}, s32[256]{0:T(256)S(1)}, u32[]{:S(2)}) copy-start(s32[256]{0:T(256)S(1)} %get-tuple-element.10.link_ref.link_hbm) | copy-start | bytes 3076
  54.0 2.2 %copy-start = (bf16[65,128,256]{2,1,0:T(8,128)(2,1)S(1)}, bf16[65,128,256]{2,1,0:T(8,128)(2,1)}, u32[]{:S(2)}) copy-start(bf16[65,128,256]{2,1,0:T(8,128)(2,1)} %get-tuple-element.12.left_ref.left_hbm) | copy-start | bytes 12779524

commit v4 on v3

--- a/solution.py
+++ b/solution.py
@@ -42,20 +42,19 @@
     return both[:, :width] + both[:, width:]
 
 
-def pick_kernel(send_ref, p_ref, below_ref, above_ref, sem):
-    def copy(side, target, j):
+def pick_kernel(side, send_ref, p_ref, out_ref, sem):
+    def copy(j):
         row = jnp.maximum(send_ref[0, side, j], 0)
-        return pltpu.make_async_copy(p_ref.at[row], target.at[j], sem.at[side, j])
-
-    targets = ((1, above_ref), (0, below_ref))
-    for side, target in targets:
-        @pl.loop(0, target.shape[0])
-        def _(j):
-            copy(side, target, j).start()
-    for side, target in targets:
-        @pl.loop(0, target.shape[0])
-        def _(j):
-            copy(side, target, j).wait()
+        return pltpu.make_async_copy(p_ref.at[row], out_ref.at[j], sem.at[j])
+
+    @pl.loop(0, out_ref.shape[0] // 4)
+    def _(g):
+        for i in range(4):
+            copy(g * 4 + i).start()
+
+    @pl.loop(0, out_ref.shape[0])
+    def _(j):
+        copy(j).wait()
 
 
 def local_kernel(col_ref, tile_ref, p_ref, a_ref, sum_ref, left_ref, link_ref, right_p, place_ref):
@@ -110,22 +109,7 @@
                 link_ref[slots + t] = j
 
 
-def lower_kernel(link_ref, left_ref, lower_ref, chain_ref):
-    group = lower_ref.shape[0]
-    capacity = chain_ref.shape[0] - 1
-    step = pl.program_id(0)
-
-    @pl.when(step == 0)
-    def _():
-        chain_ref[capacity] = jnp.zeros(chain_ref.shape[1:], jnp.float32)
-
-    for i in range(group):
-        slot = step * group + i
-        triple = product(left_ref[i], right_form(lower_ref[i]))
-        chain_ref[slot] = triple + chain_ref[jnp.minimum(link_ref[slot], capacity)]
-
-
-def reduce_kernel(orders, link_hbm, part_ref, left_hbm, lower_hbm, upper, out_ref, link_ref, left, mine, chain, *rest):
+def reduce_kernel(orders, link_hbm, part_ref, left_hbm, lower, upper, out_ref, link_ref, left, mine, chain, *rest):
     stages = len(orders[0])
     bufs = rest[:stages]
     load_sem, halo_sem, send_sem, recv_sem = rest[stages:]
@@ -133,8 +117,8 @@
     tiles = part_ref.shape[0]
     chunks = load_sem.shape[0]
     capacity = upper.shape[0]
-    pieces = capacity // PIECE
     slots = 2 * capacity
+    pieces = slots // PIECE
     width = tiles // chunks
     ways = len(orders)
     bit = [(me // 2**b) % 2 for b in range(stages)]
@@ -196,17 +180,14 @@
                 body(g * ways + way, way)
 
     link_load = pltpu.make_async_copy(link_hbm, link_ref, halo_sem.at[pieces])
-    lower_load = pltpu.make_async_copy(
-        lower_hbm.at[pl.ds(0, capacity)], chain.at[pl.ds(0, capacity)], halo_sem.at[pieces + 1])
 
     def left_load(g):
         return pltpu.make_async_copy(
-            left_hbm.at[pl.ds(capacity + g * PIECE, PIECE)], left.at[pl.ds(g * PIECE, PIECE)], halo_sem.at[g])
+            left_hbm.at[pl.ds(g * PIECE, PIECE)], left.at[pl.ds(g * PIECE, PIECE)], halo_sem.at[g])
 
     link_load.start()
     for g in range(pieces):
         left_load(g).start()
-    lower_load.start()
     each(lambda c, way: load(c, way).start())
     barrier = pltpu.get_barrier_semaphore()
     for b in range(stages):
@@ -214,15 +195,16 @@
 
     chain[slots] = jnp.zeros(chain.shape[1:], jnp.float32)
     link_load.wait()
-    lower_load.wait()
-
-    @pl.loop(0, pieces)
-    def _(g):
-        left_load(g).wait()
-        for i in range(PIECE):
-            j = g * PIECE + i
-            triple = product(left[j], right_form(upper[j]))
-            chain[capacity + j] = triple + chain[link_ref[capacity + j]]
+
+    for side, arrived in enumerate((lower, upper)):
+        @pl.loop(0, capacity // PIECE)
+        def _(g, side=side, arrived=arrived):
+            left_load(side * (capacity // PIECE) + g).wait()
+            for i in range(PIECE):
+                j = g * PIECE + i
+                slot = side * capacity + j
+                triple = product(left[slot], right_form(arrived[j]))
+                chain[slot] = triple + chain[link_ref[slot]]
 
     pl.semaphore_wait(barrier, stages)
 
@@ -273,22 +255,23 @@
         orders = (bits, bits[stages // 2:] + bits[:stages // 2])
     tile = (rows, columns)
     hbm_spec = pl.BlockSpec(memory_space=pltpu.HBM)
+    vmem_spec = pl.BlockSpec(memory_space=pltpu.VMEM)
     vmem = functools.partial(pltpu.VMEM, dtype=jnp.float32)
     return pl.pallas_call(
         functools.partial(reduce_kernel, orders),
         out_shape=pltpu.VMEM(partial.shape, jnp.float32),
-        in_specs=[hbm_spec] * 4 + [pl.BlockSpec(memory_space=pltpu.VMEM)],
-        out_specs=pl.BlockSpec(memory_space=pltpu.VMEM),
+        in_specs=[hbm_spec] * 3 + [vmem_spec] * 2,
+        out_specs=vmem_spec,
         scratch_shapes=[
             pltpu.SMEM(links.shape, jnp.int32),
-            pltpu.VMEM((capacity,) + left.shape[1:], left.dtype),
+            pltpu.VMEM((2 * capacity,) + left.shape[1:], left.dtype),
             vmem(partial.shape),
             vmem((2 * capacity + 1,) + tile),
         ]
         + [vmem((chunks, width >> (s + 1)) + tile) for s in range(stages)]
         + [
             pltpu.SemaphoreType.DMA((chunks,)),
-            pltpu.SemaphoreType.DMA((capacity // PIECE + 2,)),
+            pltpu.SemaphoreType.DMA((2 * capacity // PIECE + 1,)),
             pltpu.SemaphoreType.DMA((2 * stages, chunks)),
             pltpu.SemaphoreType.DMA((2 * stages, chunks)),
         ],
@@ -309,18 +292,19 @@
     vmem_spec = pl.BlockSpec(memory_space=pltpu.VMEM)
     hbm_spec = pl.BlockSpec(memory_space=pltpu.HBM)
 
-    sent = pltpu.VMEM((capacity,) + tile, jnp.float32)
-    to_below, to_above = pl.pallas_call(
-        pick_kernel,
-        out_shape=(sent, sent),
-        in_specs=[smem_spec, hbm_spec],
-        out_specs=(vmem_spec, vmem_spec),
-        scratch_shapes=[pltpu.SemaphoreType.DMA((2, capacity))],
-        compiler_params=pltpu.CompilerParams(vmem_limit_bytes=8 * 1024 * 1024),
-        name="pick",
-    )(send_list, pltpu.with_memory_space_constraint(p_tiles, pltpu.HBM))
-    lower = shifted(to_above, ("group", "bulk"), 1)
-    upper = shifted(to_below, ("group", "bulk"), -1)
+    def picked(side, name):
+        return pl.pallas_call(
+            functools.partial(pick_kernel, side),
+            out_shape=pltpu.VMEM((capacity,) + tile, jnp.float32),
+            in_specs=[smem_spec, hbm_spec],
+            out_specs=vmem_spec,
+            scratch_shapes=[pltpu.SemaphoreType.DMA((capacity,))],
+            compiler_params=pltpu.CompilerParams(vmem_limit_bytes=8 * 1024 * 1024),
+            name=name,
+        )(send_list, pltpu.with_memory_space_constraint(p_tiles, pltpu.HBM))
+
+    lower = shifted(picked(1, "pick_above"), ("group", "bulk"), 1)
+    upper = shifted(picked(0, "pick_below"), ("group", "bulk"), -1)
 
     couplings = blocks * neighbours
     whole = lambda *shape: pl.BlockSpec(shape, lambda s, *_: (0,) * len(shape))
@@ -347,24 +331,8 @@
         name="local_products",
     )(col_ref.T, coarse_tile.T, p_tiles, a_tiles)
 
-    lower_chain = pl.pallas_call(
-        lower_kernel,
-        out_shape=pltpu.HBM((capacity + 1,) + tile, jnp.float32),
-        grid_spec=pltpu.PrefetchScalarGridSpec(
-            num_scalar_prefetch=1,
-            grid=(capacity // PIECE,),
-            in_specs=[
-                pl.BlockSpec((PIECE, rows, 2 * columns), lambda s, *_: (s, 0, 0)),
-                pl.BlockSpec((PIECE,) + tile, lambda s, *_: (s, 0, 0)),
-            ],
-            out_specs=whole(capacity + 1, *tile),
-        ),
-        compiler_params=pltpu.CompilerParams(vmem_limit_bytes=24 * 1024 * 1024),
-        cost_estimate=pl.CostEstimate(
-            flops=capacity * 8 * rows * rows * columns, bytes_accessed=12 * capacity * rows * columns, transcendentals=0),
-        name="lower_products",
-    )(links, left, lower)
-    return group_sum(links, partial, left, lower_chain, pltpu.with_memory_space_constraint(upper, pltpu.VMEM))
+    lower, upper = (pltpu.with_memory_space_constraint(x, pltpu.VMEM) for x in (lower, upper))
+    return group_sum(links, partial, left, lower, upper)
 
 
 def solution(mesh):

time: 144 us -> 138 us (0.958)
  Pallas kernels: 116 us -> 112 us
  local copies, waits for them, and re-layouts: 6.3 us -> 4.09 us
    pallas_call x2, Pallas kernels: 7.63 us -> 4.86 us  [picked(): pl.pallas_call(functools.partial(pick_kernel, side), out_shape=pltpu.VMEM...]
    unnamed x11 -> x9, local copies, waits for them, and re-layouts: 6.3 us -> 4.09 us
  transfers between devices with their start and end apart: 2 -> 2, of which waited for: 1 -> 2; matrix products, arithmetic and copies ran while one was open for 0% -> 0% of each run, Pallas kernels for 22% -> 22%
where the time goes in v4:
time: 138 us; the launch traced here: 137 us
  Pallas kernels  112 us (81%)
  waiting for transfers between devices  14.5 us (11%)
  starting transfers between devices  6.4 us (5%)
  local copies, waits for them, and re-layouts  4.09 us (3%)
    pallas_call x1, Pallas kernels, group_sum(): pl.pallas_call(functools.partial(reduce_kernel, orders), out_shape=pltpu....  79.1 us
    pallas_call x1, Pallas kernels, shards(): pl.pallas_call(local_kernel, out_shape=(jax.ShapeDtypeStruct((CT,) + tile...  28.2 us
    ppermute x2, waiting for transfers between devices, shifted(): return lax.ppermute(block, axis, route)  14.5 us
    ppermute x2, starting transfers between devices, shifted(): return lax.ppermute(block, axis, route)  6.4 us
    pallas_call x2, Pallas kernels, picked(): pl.pallas_call(functools.partial(pick_kernel, side), out_shape=pltpu.VMEM...  4.86 us
    unnamed x9, local copies, waits for them, and re-layouts  4.09 us
  transfers between devices with their start and end apart: 2, of which 2 were waited for; matrix products, arithmetic and copies ran while one was open for 0% of the time, Pallas kernels for 22%

profile of v4, /device:TPU:1, one launch (start us, length us, event | category | flops | bytes accessed | tf_op | source)
XLA Modules:
  0.0 137.2 jit_solution(15493304141303603796)
XLA Ops:
  0.0 0.0 copy-start
  0.0 0.7 copy-done
  0.7 0.0 copy-start.2
  0.7 0.0 copy-start.3
  0.7 2.4 %pick_above.1 = f32[32,128,128]{2,1,0:T(8,128)S(1)} custom-call(s32[1,2,32]{2,1,0:T(2,128)S(1)} %copy-done, f32[48,128,128]{2,1,0:T(8,128)} %p_ref.5), custom_call_target="tpu_custom_call" | custom-call | tf_op jit(solution)/shard_map/pick_above/pallas_call | solution.py:296
  3.1 4.5 %collective-permute-start = (f32[32,128,128]{2,1,0:T(8,128)S(1)}, f32[32,128,128]{2,1,0:T(8,128)S(1)}, u32[]{:S(2)}, u32[]{:S(2)}) collective-permute-start(f32[32,128,128]{2,1,0:T(8,128)S(1)} %pick_above.1), channel_id=1, source_target_pairs={{0,1},{1,2},{2,3},{3,4},{4,5},{5,6},{6,7},{7,8},{8,9},{9,10},{10,1... | collective-permute-start | bytes 6291464 | tf_op jit(solution)/shard_map/ppermute | solution.py:21
  7.6 2.4 %pick_below.1 = f32[32,128,128]{2,1,0:T(8,128)S(1)} custom-call(s32[1,2,32]{2,1,0:T(2,128)S(1)} %copy-done, f32[48,128,128]{2,1,0:T(8,128)} %p_ref.5), custom_call_target="tpu_custom_call" | custom-call | tf_op jit(solution)/shard_map/pick_below/pallas_call | solution.py:296
  10.0 1.9 %collective-permute-start.1 = (f32[32,128,128]{2,1,0:T(8,128)S(1)}, f32[32,128,128]{2,1,0:T(8,128)S(1)}, u32[]{:S(2)}, u32[]{:S(2)}) collective-permute-start(f32[32,128,128]{2,1,0:T(8,128)S(1)} %pick_below.1), channel_id=1, source_target_pairs={{1,0},{2,1},{3,2},{4,3},{5,4},{6,5},{7,6},{8,7},{9,8},{10,9},{11,1... | collective-permute-start | bytes 6291464 | tf_op jit(solution)/shard_map/ppermute | solution.py:21
  12.0 0.0 copy-done.2
  12.0 0.0 copy-done.3
  12.0 28.2 %local_products.1 = (f32[128,128,128]{2,1,0:T(8,128)}, bf16[65,128,256]{2,1,0:T(8,128)(2,1)}, s32[256]{0:T(256)S(1)}) custom-call(s32[7,48]{1,0:T(8,128)S(1)} %bitcast.2, s32[7,48]{1,0:T(8,128)S(1)} %bitcast.3, f32[48,128,128]{2,1,0:T(8,128)} %p_ref.5, f32[48,7,128,128]{3,2,1,0:T(8,128)} %a_ref.1), custom_call_target="tpu_custom_call" | custom-call | flops 11274289152 | bytes 22020096 | tf_op jit(solution)/shard_map/local_products/pallas_call | solution.py:311
  40.2 0.0 copy-start.1
  40.2 12.8 %collective-permute-done.lower = f32[32,128,128]{2,1,0:T(8,128)S(1)} collective-permute-done((f32[32,128,128]{2,1,0:T(8,128)S(1)}, f32[32,128,128]{2,1,0:T(8,128)S(1)}, u32[]{:S(2)}, u32[]{:S(2)}) %collective-permute-start) | collective-permute-done | bytes 2097184 | tf_op jit(solution)/shard_map/ppermute | solution.py:21
  53.1 1.6 %collective-permute-done.1.upper = f32[32,128,128]{2,1,0:T(8,128)S(1)} collective-permute-done((f32[32,128,128]{2,1,0:T(8,128)S(1)}, f32[32,128,128]{2,1,0:T(8,128)S(1)}, u32[]{:S(2)}, u32[]{:S(2)}) %collective-permute-start.1) | collective-permute-done | bytes 2097184 | tf_op jit(solution)/shard_map/ppermute | solution.py:21
  54.7 0.0 copy-done.1
  54.7 79.1 %group_sum.1 = f32[128,128,128]{2,1,0:T(8,128)S(1)} custom-call(s32[256]{0:T(256)} %copy-done.1, f32[128,128,128]{2,1,0:T(8,128)} %get-tuple-element.9.part_ref, bf16[65,128,256]{2,1,0:T(8,128)(2,1)} %get-tuple-element.10.left_hbm, f32[32,128,128]{2,1,0:T(8,128)S(1)} %collective-permute-done.lower, f32[32,128,128]{2,1,0:T(8,128)S(1)} %collective-permute-done.1.upper), custom_call_target="tpu_custom_call" | custom-call | flops 2097152 | bytes 16777216 | tf_op jit(solution)/shard_map/group_sum/pallas_call | solution.py:260
  133.8 3.4 %copy.7 = f32[128,128,128]{2,1,0:T(8,128)} copy(f32[128,128,128]{2,1,0:T(8,128)S(1)} %group_sum.1) | data formatting | bytes 16777216
Async XLA Ops:
  0.0 0.7 copy-start
  0.7 11.3 %copy-start.2 = (s32[48,7]{0,1:T(8,128)S(1)}, s32[48,7]{0,1:T(8,128)}, u32[]{:S(2)}) copy-start(s32[48,7]{0,1:T(8,128)} %param.7) | copy-start | bytes 4036
  0.7 11.3 %copy-start.3 = (s32[48,7]{0,1:T(8,128)S(1)}, s32[48,7]{0,1:T(8,128)}, u32[]{:S(2)}) copy-start(s32[48,7]{0,1:T(8,128)} %param.9) | copy-start | bytes 4036
  3.1 49.9 %collective-permute-start = (f32[32,128,128]{2,1,0:T(8,128)S(1)}, f32[32,128,128]{2,1,0:T(8,128)S(1)}, u32[]{:S(2)}, u32[]{:S(2)}) collective-permute-start(f32[32,128,128]{2,1,0:T(8,128)S(1)} %pick_above.1), channel_id=1, source_target_pairs={{0,1},{1,2},{2,3},{3,4},{4,5},{5,6},{6,7},{7,8},{8,9},{9,10},{10,1... | collective-permute-start | bytes 6291464 | tf_op jit(solution)/shard_map/ppermute | solution.py:21
  10.0 44.7 %collective-permute-start.1 = (f32[32,128,128]{2,1,0:T(8,128)S(1)}, f32[32,128,128]{2,1,0:T(8,128)S(1)}, u32[]{:S(2)}, u32[]{:S(2)}) collective-permute-start(f32[32,128,128]{2,1,0:T(8,128)S(1)} %pick_below.1), channel_id=1, source_target_pairs={{1,0},{2,1},{3,2},{4,3},{5,4},{6,5},{7,6},{8,7},{9,8},{10,9},{11,1... | collective-permute-start | bytes 6291464 | tf_op jit(solution)/shard_map/ppermute | solution.py:21
  40.2 14.5 %copy-start.1 = (s32[256]{0:T(256)}, s32[256]{0:T(256)S(1)}, u32[]{:S(2)}) copy-start(s32[256]{0:T(256)S(1)} %get-tuple-element.8.link_hbm) | copy-start | bytes 3076

commit v5 on v4

--- a/solution.py
+++ b/solution.py
@@ -161,8 +161,7 @@
         size = width >> (s + 1)
         at, _ = keep(c, way, s)
 
-        @pl.loop(0, size)
-        def _(j):
+        def add_tile(j):
             if s == 0:
                 own = mine[c * width + bit[b] * size + j]
             else:
@@ -173,6 +172,14 @@
             else:
                 bufs[s][c, j] = total
 
+        if size % 2:
+            pl.loop(0, size)(add_tile)
+        else:
+            @pl.loop(0, size // 2)
+            def _(g):
+                add_tile(2 * g)
+                add_tile(2 * g + 1)
+
     def each(body):
         @pl.loop(0, chunks // ways)
         def _(g):
@@ -211,21 +218,35 @@
     def finish(c, way):
         load(c, way).wait()
 
-        @pl.loop(0, width)
-        def _(i):
-            t = c * width + i
-            mine[t] += chain[link_ref[slots + t]]
+        @pl.loop(0, width // 4)
+        def _(g):
+            for i in range(4):
+                t = c * width + g * 4 + i
+                mine[t] += chain[link_ref[slots + t]]
         scatter(c, way, 0).start()
-    each(finish)
-    for s in range(stages):
-        def reduce_step(c, way, s=s):
-            scatter(c, way, s).wait_recv()
-            add(c, way, s)
-            if s + 1 < stages:
-                scatter(c, way, s + 1).start()
-            else:
-                gather(c, way, s).start()
-        each(reduce_step)
+
+    def reduce_step(c, way, s):
+        scatter(c, way, s).wait_recv()
+        add(c, way, s)
+        if s + 1 < stages:
+            scatter(c, way, s + 1).start()
+        else:
+            gather(c, way, s).start()
+
+    for way in range(ways):
+        finish(way, way)
+
+    @pl.loop(1, chunks // ways)
+    def _(g):
+        for way in range(ways):
+            finish(g * ways + way, way)
+        for way in range(ways):
+            reduce_step((g - 1) * ways + way, way, 0)
+
+    for way in range(ways):
+        reduce_step(chunks - ways + way, way, 0)
+    for s in range(1, stages):
+        each(functools.partial(reduce_step, s=s))
     for s in reversed(range(stages)):
         def spread_step(c, way, s=s):
             gather(c, way, s).wait_recv()

time: 138 us -> 137 us (level)
  transfers between devices with their start and end apart: 2 -> 2, of which waited for: 2 -> 2; matrix products, arithmetic and copies ran while one was open for 0% -> 0% of each run, Pallas kernels for 22% -> 23%
where the time goes in v5:
time: 137 us; the launch traced here: 136 us
  Pallas kernels  111 us (81%)
  waiting for transfers between devices  14.3 us (10%)
  starting transfers between devices  6.43 us (5%)
  local copies, waits for them, and re-layouts  4.09 us (3%)
    pallas_call x1, Pallas kernels, group_sum(): pl.pallas_call(functools.partial(reduce_kernel, orders), out_shape=pltpu....  78 us
    pallas_call x1, Pallas kernels, shards(): pl.pallas_call(local_kernel, out_shape=(jax.ShapeDtypeStruct((CT,) + tile...  28.2 us
    ppermute x2, waiting for transfers between devices, shifted(): return lax.ppermute(block, axis, route)  14.3 us
    ppermute x2, starting transfers between devices, shifted(): return lax.ppermute(block, axis, route)  6.43 us
    pallas_call x2, Pallas kernels, picked(): pl.pallas_call(functools.partial(pick_kernel, side), out_shape=pltpu.VMEM...  5.21 us
    unnamed x9, local copies, waits for them, and re-layouts  4.09 us
  transfers between devices with their start and end apart: 2, of which 2 were waited for; matrix products, arithmetic and copies ran while one was open for 0% of the time, Pallas kernels for 23%

profile of v5, /device:TPU:1, one launch (start us, length us, event | category | flops | bytes accessed | tf_op | source)
XLA Modules:
  0.0 136.3 jit_solution(8664375148918843996)
XLA Ops:
  0.0 0.0 copy-start
  0.0 0.7 copy-done
  0.7 0.0 copy-start.2
  0.7 0.0 copy-start.3
  0.7 2.4 %pick_above.1 = f32[32,128,128]{2,1,0:T(8,128)S(1)} custom-call(s32[1,2,32]{2,1,0:T(2,128)S(1)} %copy-done, f32[48,128,128]{2,1,0:T(8,128)} %p_ref.5), custom_call_target="tpu_custom_call" | custom-call | tf_op jit(solution)/shard_map/pick_above/pallas_call | solution.py:317
  3.1 4.5 %collective-permute-start = (f32[32,128,128]{2,1,0:T(8,128)S(1)}, f32[32,128,128]{2,1,0:T(8,128)S(1)}, u32[]{:S(2)}, u32[]{:S(2)}) collective-permute-start(f32[32,128,128]{2,1,0:T(8,128)S(1)} %pick_above.1), channel_id=1, source_target_pairs={{0,1},{1,2},{2,3},{3,4},{4,5},{5,6},{6,7},{7,8},{8,9},{9,10},{10,1... | collective-permute-start | bytes 6291464 | tf_op jit(solution)/shard_map/ppermute | solution.py:21
  7.6 2.8 %pick_below.1 = f32[32,128,128]{2,1,0:T(8,128)S(1)} custom-call(s32[1,2,32]{2,1,0:T(2,128)S(1)} %copy-done, f32[48,128,128]{2,1,0:T(8,128)} %p_ref.5), custom_call_target="tpu_custom_call" | custom-call | tf_op jit(solution)/shard_map/pick_below/pallas_call | solution.py:317
  10.4 1.9 %collective-permute-start.1 = (f32[32,128,128]{2,1,0:T(8,128)S(1)}, f32[32,128,128]{2,1,0:T(8,128)S(1)}, u32[]{:S(2)}, u32[]{:S(2)}) collective-permute-start(f32[32,128,128]{2,1,0:T(8,128)S(1)} %pick_below.1), channel_id=1, source_target_pairs={{1,0},{2,1},{3,2},{4,3},{5,4},{6,5},{7,6},{8,7},{9,8},{10,9},{11,1... | collective-permute-start | bytes 6291464 | tf_op jit(solution)/shard_map/ppermute | solution.py:21
  12.4 0.0 copy-done.2
  12.4 0.0 copy-done.3
  12.4 28.2 %local_products.1 = (f32[128,128,128]{2,1,0:T(8,128)}, bf16[65,128,256]{2,1,0:T(8,128)(2,1)}, s32[256]{0:T(256)S(1)}) custom-call(s32[7,48]{1,0:T(8,128)S(1)} %bitcast.2, s32[7,48]{1,0:T(8,128)S(1)} %bitcast.3, f32[48,128,128]{2,1,0:T(8,128)} %p_ref.5, f32[48,7,128,128]{3,2,1,0:T(8,128)} %a_ref.1), custom_call_target="tpu_custom_call" | custom-call | flops 11274289152 | bytes 22020096 | tf_op jit(solution)/shard_map/local_products/pallas_call | solution.py:332
  40.6 0.0 copy-start.1
  40.6 12.5 %collective-permute-done.lower = f32[32,128,128]{2,1,0:T(8,128)S(1)} collective-permute-done((f32[32,128,128]{2,1,0:T(8,128)S(1)}, f32[32,128,128]{2,1,0:T(8,128)S(1)}, u32[]{:S(2)}, u32[]{:S(2)}) %collective-permute-start) | collective-permute-done | bytes 2097184 | tf_op jit(solution)/shard_map/ppermute | solution.py:21
  53.1 1.9 %collective-permute-done.1.upper = f32[32,128,128]{2,1,0:T(8,128)S(1)} collective-permute-done((f32[32,128,128]{2,1,0:T(8,128)S(1)}, f32[32,128,128]{2,1,0:T(8,128)S(1)}, u32[]{:S(2)}, u32[]{:S(2)}) %collective-permute-start.1) | collective-permute-done | bytes 2097184 | tf_op jit(solution)/shard_map/ppermute | solution.py:21
  54.9 0.0 copy-done.1
  54.9 78.0 %group_sum.1 = f32[128,128,128]{2,1,0:T(8,128)S(1)} custom-call(s32[256]{0:T(256)} %copy-done.1, f32[128,128,128]{2,1,0:T(8,128)} %get-tuple-element.9.part_ref, bf16[65,128,256]{2,1,0:T(8,128)(2,1)} %get-tuple-element.10.left_hbm, f32[32,128,128]{2,1,0:T(8,128)S(1)} %collective-permute-done.lower, f32[32,128,128]{2,1,0:T(8,128)S(1)} %collective-permute-done.1.upper), custom_call_target="tpu_custom_call" | custom-call | flops 2097152 | bytes 16777216 | tf_op jit(solution)/shard_map/group_sum/pallas_call | solution.py:281
  132.9 3.4 %copy.7 = f32[128,128,128]{2,1,0:T(8,128)} copy(f32[128,128,128]{2,1,0:T(8,128)S(1)} %group_sum.1) | data formatting | bytes 16777216
Async XLA Ops:
  0.0 0.7 copy-start
  0.7 11.7 %copy-start.2 = (s32[48,7]{0,1:T(8,128)S(1)}, s32[48,7]{0,1:T(8,128)}, u32[]{:S(2)}) copy-start(s32[48,7]{0,1:T(8,128)} %param.7) | copy-start | bytes 4036
  0.7 11.7 %copy-start.3 = (s32[48,7]{0,1:T(8,128)S(1)}, s32[48,7]{0,1:T(8,128)}, u32[]{:S(2)}) copy-start(s32[48,7]{0,1:T(8,128)} %param.9) | copy-start | bytes 4036
  3.1 49.9 %collective-permute-start = (f32[32,128,128]{2,1,0:T(8,128)S(1)}, f32[32,128,128]{2,1,0:T(8,128)S(1)}, u32[]{:S(2)}, u32[]{:S(2)}) collective-permute-start(f32[32,128,128]{2,1,0:T(8,128)S(1)} %pick_above.1), channel_id=1, source_target_pairs={{0,1},{1,2},{2,3},{3,4},{4,5},{5,6},{6,7},{7,8},{8,9},{9,10},{10,1... | collective-permute-start | bytes 6291464 | tf_op jit(solution)/shard_map/ppermute | solution.py:21
  10.4 44.5 %collective-permute-start.1 = (f32[32,128,128]{2,1,0:T(8,128)S(1)}, f32[32,128,128]{2,1,0:T(8,128)S(1)}, u32[]{:S(2)}, u32[]{:S(2)}) collective-permute-start(f32[32,128,128]{2,1,0:T(8,128)S(1)} %pick_below.1), channel_id=1, source_target_pairs={{1,0},{2,1},{3,2},{4,3},{5,4},{6,5},{7,6},{8,7},{9,8},{10,9},{11,1... | collective-permute-start | bytes 6291464 | tf_op jit(solution)/shard_map/ppermute | solution.py:21
  40.6 14.3 %copy-start.1 = (s32[256]{0:T(256)}, s32[256]{0:T(256)S(1)}, u32[]{:S(2)}) copy-start(s32[256]{0:T(256)S(1)} %get-tuple-element.8.link_hbm) | copy-start | bytes 3076

commit v6 on v5

--- a/solution.py
+++ b/solution.py
@@ -42,19 +42,14 @@
     return both[:, :width] + both[:, width:]
 
 
-def pick_kernel(side, send_ref, p_ref, out_ref, sem):
-    def copy(j):
+def pick_kernel(side, send_hbm, p_ref, out_ref, send_ref, list_sem, sem):
+    fetch = pltpu.make_async_copy(send_hbm, send_ref, list_sem)
+    fetch.start()
+    fetch.wait()
+    for j in range(out_ref.shape[0]):
         row = jnp.maximum(send_ref[0, side, j], 0)
-        return pltpu.make_async_copy(p_ref.at[row], out_ref.at[j], sem.at[j])
-
-    @pl.loop(0, out_ref.shape[0] // 4)
-    def _(g):
-        for i in range(4):
-            copy(g * 4 + i).start()
-
-    @pl.loop(0, out_ref.shape[0])
-    def _(j):
-        copy(j).wait()
+        pltpu.make_async_copy(p_ref.at[row], out_ref.at[j], sem).start()
+    pltpu.make_async_copy(p_ref.at[pl.ds(0, out_ref.shape[0])], out_ref, sem).wait()
 
 
 def local_kernel(col_ref, tile_ref, p_ref, a_ref, sum_ref, left_ref, link_ref, right_p, place_ref):
@@ -317,12 +312,12 @@
         return pl.pallas_call(
             functools.partial(pick_kernel, side),
             out_shape=pltpu.VMEM((capacity,) + tile, jnp.float32),
-            in_specs=[smem_spec, hbm_spec],
+            in_specs=[hbm_spec, hbm_spec],
             out_specs=vmem_spec,
-            scratch_shapes=[pltpu.SemaphoreType.DMA((capacity,))],
+            scratch_shapes=[pltpu.SMEM(send_list.shape, jnp.int32), pltpu.SemaphoreType.DMA, pltpu.SemaphoreType.DMA],
             compiler_params=pltpu.CompilerParams(vmem_limit_bytes=8 * 1024 * 1024),
             name=name,
-        )(send_list, pltpu.with_memory_space_constraint(p_tiles, pltpu.HBM))
+        )(*(pltpu.with_memory_space_constraint(x, pltpu.HBM) for x in (send_list, p_tiles)))
 
     lower = shifted(picked(1, "pick_above"), ("group", "bulk"), 1)
     upper = shifted(picked(0, "pick_below"), ("group", "bulk"), -1)

time: 137 us -> 137 us (level)
    unnamed x9 -> x7, local copies, waits for them, and re-layouts: 4.09 us -> 3.41 us
where the time goes in v6:
time: 137 us; the launch traced here: 136 us
  Pallas kernels  111 us (81%)
  waiting for transfers between devices  14.3 us (10%)
  starting transfers between devices  6.77 us (5%)
  local copies, waits for them, and re-layouts  3.41 us (2%)
    pallas_call x1, Pallas kernels, group_sum(): pl.pallas_call(functools.partial(reduce_kernel, orders), out_shape=pltpu....  78.1 us
    pallas_call x1, Pallas kernels, shards(): pl.pallas_call(local_kernel, out_shape=(jax.ShapeDtypeStruct((CT,) + tile...  28.2 us
    ppermute x2, waiting for transfers between devices, shifted(): return lax.ppermute(block, axis, route)  14.3 us
    ppermute x2, starting transfers between devices, shifted(): return lax.ppermute(block, axis, route)  6.77 us
    pallas_call x2, Pallas kernels, picked(): pl.pallas_call(functools.partial(pick_kernel, side), out_shape=pltpu.VMEM...  5.09 us
    unnamed x7, local copies, waits for them, and re-layouts  3.41 us
  transfers between devices with their start and end apart: 2, of which 2 were waited for; matrix products, arithmetic and copies ran while one was open for 0% of the time, Pallas kernels for 23%

profile of v6, /device:TPU:1, one launch (start us, length us, event | category | flops | bytes accessed | tf_op | source)
XLA Modules:
  0.0 136.0 jit_solution(15257442847553655501)
XLA Ops:
  0.0 0.0 copy-start.2
  0.0 0.0 copy-start.1
  0.0 2.4 %pick_above.1 = f32[32,128,128]{2,1,0:T(8,128)S(1)} custom-call(s32[1,2,32]{2,1,0:T(2,128)} %send_hbm.3, f32[48,128,128]{2,1,0:T(8,128)} %p_ref.5), custom_call_target="tpu_custom_call" | custom-call | tf_op jit(solution)/shard_map/pick_above/pallas_call | solution.py:312
  2.4 4.8 %collective-permute-start = (f32[32,128,128]{2,1,0:T(8,128)S(1)}, f32[32,128,128]{2,1,0:T(8,128)S(1)}, u32[]{:S(2)}, u32[]{:S(2)}) collective-permute-start(f32[32,128,128]{2,1,0:T(8,128)S(1)} %pick_above.1), channel_id=1, source_target_pairs={{0,1},{1,2},{2,3},{3,4},{4,5},{5,6},{6,7},{7,8},{8,9},{9,10},{10,1... | collective-permute-start | bytes 6291464 | tf_op jit(solution)/shard_map/ppermute | solution.py:21
  7.3 2.7 %pick_below.1 = f32[32,128,128]{2,1,0:T(8,128)S(1)} custom-call(s32[1,2,32]{2,1,0:T(2,128)} %send_hbm.3, f32[48,128,128]{2,1,0:T(8,128)} %p_ref.5), custom_call_target="tpu_custom_call" | custom-call | tf_op jit(solution)/shard_map/pick_below/pallas_call | solution.py:312
  10.0 1.9 %collective-permute-start.1 = (f32[32,128,128]{2,1,0:T(8,128)S(1)}, f32[32,128,128]{2,1,0:T(8,128)S(1)}, u32[]{:S(2)}, u32[]{:S(2)}) collective-permute-start(f32[32,128,128]{2,1,0:T(8,128)S(1)} %pick_below.1), channel_id=1, source_target_pairs={{1,0},{2,1},{3,2},{4,3},{5,4},{6,5},{7,6},{8,7},{9,8},{10,9},{11,1... | collective-permute-start | bytes 6291464 | tf_op jit(solution)/shard_map/ppermute | solution.py:21
  11.9 0.0 copy-done.2
  11.9 0.0 copy-done.1
  11.9 28.2 %local_products.1 = (f32[128,128,128]{2,1,0:T(8,128)}, bf16[65,128,256]{2,1,0:T(8,128)(2,1)}, s32[256]{0:T(256)S(1)}) custom-call(s32[7,48]{1,0:T(8,128)S(1)} %bitcast.2, s32[7,48]{1,0:T(8,128)S(1)} %bitcast.3, f32[48,128,128]{2,1,0:T(8,128)} %p_ref.5, f32[48,7,128,128]{3,2,1,0:T(8,128)} %a_ref.1), custom_call_target="tpu_custom_call" | custom-call | flops 11274289152 | bytes 22020096 | tf_op jit(solution)/shard_map/local_products/pallas_call | solution.py:327
  40.1 0.0 copy-start
  40.1 12.5 %collective-permute-done.lower = f32[32,128,128]{2,1,0:T(8,128)S(1)} collective-permute-done((f32[32,128,128]{2,1,0:T(8,128)S(1)}, f32[32,128,128]{2,1,0:T(8,128)S(1)}, u32[]{:S(2)}, u32[]{:S(2)}) %collective-permute-start) | collective-permute-done | bytes 2097184 | tf_op jit(solution)/shard_map/ppermute | solution.py:21
  52.7 1.7 %collective-permute-done.1.upper = f32[32,128,128]{2,1,0:T(8,128)S(1)} collective-permute-done((f32[32,128,128]{2,1,0:T(8,128)S(1)}, f32[32,128,128]{2,1,0:T(8,128)S(1)}, u32[]{:S(2)}, u32[]{:S(2)}) %collective-permute-start.1) | collective-permute-done | bytes 2097184 | tf_op jit(solution)/shard_map/ppermute | solution.py:21
  54.4 0.0 copy-done
  54.4 78.1 %group_sum.1 = f32[128,128,128]{2,1,0:T(8,128)S(1)} custom-call(s32[256]{0:T(256)} %copy-done, f32[128,128,128]{2,1,0:T(8,128)} %get-tuple-element.9.part_ref, bf16[65,128,256]{2,1,0:T(8,128)(2,1)} %get-tuple-element.10.left_hbm, f32[32,128,128]{2,1,0:T(8,128)S(1)} %collective-permute-done.lower, f32[32,128,128]{2,1,0:T(8,128)S(1)} %collective-permute-done.1.upper), custom_call_target="tpu_custom_call" | custom-call | flops 2097152 | bytes 16777216 | tf_op jit(solution)/shard_map/group_sum/pallas_call | solution.py:276
  132.6 3.4 %copy.7 = f32[128,128,128]{2,1,0:T(8,128)} copy(f32[128,128,128]{2,1,0:T(8,128)S(1)} %group_sum.1) | data formatting | bytes 16777216
Async XLA Ops:
  0.0 11.9 %copy-start.2 = (s32[48,7]{0,1:T(8,128)S(1)}, s32[48,7]{0,1:T(8,128)}, u32[]{:S(2)}) copy-start(s32[48,7]{0,1:T(8,128)} %param.9) | copy-start | bytes 4036
  0.0 11.9 %copy-start.1 = (s32[48,7]{0,1:T(8,128)S(1)}, s32[48,7]{0,1:T(8,128)}, u32[]{:S(2)}) copy-start(s32[48,7]{0,1:T(8,128)} %param.7) | copy-start | bytes 4036
  2.4 50.3 %collective-permute-start = (f32[32,128,128]{2,1,0:T(8,128)S(1)}, f32[32,128,128]{2,1,0:T(8,128)S(1)}, u32[]{:S(2)}, u32[]{:S(2)}) collective-permute-start(f32[32,128,128]{2,1,0:T(8,128)S(1)} %pick_above.1), channel_id=1, source_target_pairs={{0,1},{1,2},{2,3},{3,4},{4,5},{5,6},{6,7},{7,8},{8,9},{9,10},{10,1... | collective-permute-start | bytes 6291464 | tf_op jit(solution)/shard_map/ppermute | solution.py:21
  10.0 44.4 %collective-permute-start.1 = (f32[32,128,128]{2,1,0:T(8,128)S(1)}, f32[32,128,128]{2,1,0:T(8,128)S(1)}, u32[]{:S(2)}, u32[]{:S(2)}) collective-permute-start(f32[32,128,128]{2,1,0:T(8,128)S(1)} %pick_below.1), channel_id=1, source_target_pairs={{1,0},{2,1},{3,2},{4,3},{5,4},{6,5},{7,6},{8,7},{9,8},{10,9},{11,1... | collective-permute-start | bytes 6291464 | tf_op jit(solution)/shard_map/ppermute | solution.py:21
  40.1 14.3 %copy-start = (s32[256]{0:T(256)}, s32[256]{0:T(256)S(1)}, u32[]{:S(2)}) copy-start(s32[256]{0:T(256)S(1)} %get-tuple-element.8.link_hbm) | copy-start | bytes 3076
